TPU v7x, 512 devices: a whole 4x4x16 slice. The times are simulated.
512 devices in a mesh: seq: 128 (over y, z, core), head: 4 (over x).
Axes of the slice: x: 4, y: 4, z: 16, core: 2. Of those that a mesh axis runs over, the one named last changes fastest.
Arguments:
- queries: bfloat16 [32768, 2048], P('seq', 'head'), may hold values from -6 to 6
- keys: bfloat16 [32768, 2048], P('seq', 'head'), may hold values from -40 to 40
- values: bfloat16 [32768, 2048], P('seq', 'head'), may hold values from -24 to 24
- ridges: float32 [16], P('head'), may hold values from 0.25 to 4
- out_weight: bfloat16 [2048, 2048], P('head'), may hold values from -0.125 to 0.125
Outputs:
- layer_out: bfloat16 [32768, 2048], P('seq', 'head')
All inputs are finite; a program needn't handle non-finite values.
Results may differ from a plain program's by a relative error of at most 0.0049.
Values may be sent and summed in bfloat16 or wider, within the bound.
No kernel may reach another device: no remote copies, remote signals or barrier semaphores. Data moves between devices by JAX's collectives and lax.ppermute only.
A program may use at most 128 MiB of HBM per device.

v0:
```python
import jax
import jax.numpy as jnp
from jax import lax
from jax.sharding import Mesh
from jax.sharding import PartitionSpec as P

HD = 128
SPAN = 128
ITERS = 2
SEQ = ("seq_0", "seq_1", "seq_2")


highest = lax.Precision.HIGHEST


def neutral_like(value, identity):
    return jax.tree.map(
        lambda part, zero: jnp.zeros_like(part) + jnp.asarray(zero, part.dtype), value, identity
    )


def entering(value, axes, combine, identity):
    before = start = neutral_like(value, identity)
    total = value
    for axis in reversed(axes):
        length, mine = (lax.axis_size(axis), lax.axis_index(axis))
        pieces = jax.tree.map(lambda part: lax.all_gather(part, axis), total)
        inside, total = (start, start)
        for k in range(length):
            passed = k < mine
            total = combine(total, jax.tree.map(lambda part: part[k], pieces))
            inside = jax.tree.map(lambda new, old: jnp.where(passed, new, old), total, inside)
        before = combine(inside, before)
    return before


def copy_for_each(value, axis):
    length = lax.axis_size(axis)
    return lax.all_to_all(
        jnp.broadcast_to(value[None], (length, *value.shape)), axis, 0, 0, tiled=True
    )


def laid_out(pieces, dim):
    shape = list(pieces.shape[1:])
    shape[dim] *= pieces.shape[0]
    return jnp.moveaxis(pieces, 0, dim).reshape(shape)


def collect(value, axis, dim):
    pieces = copy_for_each(value, axis)
    return laid_out(pieces, dim)


def normalize(entries):
    return entries * lax.rsqrt(jnp.sum(entries * entries, axis=-1, keepdims=True) + 1e-06)


def split_heads(source, head_count):
    tokens = source.shape[0]
    return source.astype(jnp.float32).reshape(tokens, head_count, -1).transpose(1, 0, 2)


def add_states(earlier, later):
    return (earlier[0] + later[0], earlier[1] + later[1])


def solve_block(queries_b, keyrows, values_b, key_states, value_states, ridges):
    block_len = queries_b.shape[1]
    causal = (
        lax.broadcasted_iota(jnp.int32, (block_len, block_len), 0)
        >= lax.broadcasted_iota(jnp.int32, (block_len, block_len), 1)
    ).astype(jnp.float32)

    def within(inputs, payload):
        scores = jnp.einsum("hck,hsk->hcs", inputs, keyrows, precision=highest) * causal
        return jnp.einsum("hcs,hsk->hck", scores, payload, precision=highest)

    def with_states(inputs, matrices):
        summed = jnp.einsum("hck,hkl->hcl", inputs, matrices[0], precision=highest)
        return summed

    estimate = jnp.zeros_like(queries_b)
    residual = queries_b
    direction = queries_b
    res_norm = jnp.sum(residual * residual, axis=-1, keepdims=True)
    for sweep in range(ITERS):
        applied = (
            ridges[:, None, None] * direction
            + within(direction, keyrows)
            + with_states(direction, key_states)
        )
        step_size = res_norm / (jnp.sum(direction * applied, axis=-1, keepdims=True) + 1e-06)
        estimate = estimate + step_size * direction
        residual = residual - step_size * applied
        fresh = jnp.sum(residual * residual, axis=-1, keepdims=True)
        direction = residual + fresh / (res_norm + 1e-06) * direction
        res_norm = fresh
    return with_states(estimate, value_states) + within(estimate, values_b)


def shards(queries, keys, values, ridges, out_weight):
    head_count = ridges.shape[0]
    tokens = queries.shape[0]
    blocks = tokens // SPAN
    queries_b = normalize(split_heads(queries, head_count)).reshape(head_count, blocks, SPAN, HD)
    keys_b = normalize(split_heads(keys, head_count)).reshape(head_count, blocks, SPAN, HD)
    values_b = split_heads(values, head_count).reshape(head_count, blocks, SPAN, HD)
    key_grams = jnp.einsum("hbck,hbcl->hbkl", keys_b, keys_b, precision=highest)
    value_grams = jnp.einsum("hbck,hbcl->hbkl", keys_b, values_b, precision=highest)
    empty = jnp.zeros((head_count, HD, HD), jnp.float32)
    remote_k, remote_v = entering(
        (jnp.sum(key_grams, axis=1), jnp.sum(value_grams, axis=1)), SEQ, add_states, (empty, empty)
    )
    local_k = empty
    local_v = empty
    results = []
    for position in range(blocks):
        key_states = (remote_k + local_k,)
        value_states = (remote_v + local_v,)
        results.append(
            solve_block(
                queries_b[:, position],
                keys_b[:, position],
                values_b[:, position],
                key_states,
                value_states,
                ridges,
            )
        )
        local_k = local_k + key_grams[:, position]
        local_v = local_v + value_grams[:, position]
    mixed = (
        jnp.concatenate(results, axis=1)
        .transpose(1, 0, 2)
        .reshape(tokens, head_count * HD)
        .astype(jnp.bfloat16)
    )
    w_columns = lax.all_to_all(out_weight, "head", split_axis=1, concat_axis=0, tiled=True)
    layer_out = jnp.dot(collect(mixed, "head", 1), w_columns, preferred_element_type=jnp.float32)
    return layer_out.astype(jnp.bfloat16)


def solution(mesh):
    split = Mesh(
        mesh.devices.reshape(4, 16, 2, mesh.shape["head"]), ("seq_0", "seq_1", "seq_2", "head")
    )
    placed = (P(SEQ, "head"), P(SEQ, "head"), P(SEQ, "head"), P("head"), P("head", None))
    return jax.shard_map(
        shards, mesh=split, in_specs=placed, out_specs=P(SEQ, "head"), check_vma=False
    )
```

profile of v0, /device:TPU:1, one launch (start us, length us, event | category | flops | bytes accessed | tf_op | source)
XLA Modules:
  0.0 271.7 jit_solution(11657447770464410147)
XLA Ops:
  6.5 0.0 all-gather.13.cloned.1.call-start
  6.5 1.1 copy.82
  7.6 0.1 fusion.17
  7.8 0.2 copy.83
  8.0 0.0 copy-start.6
  8.0 1.8 fusion.72
  9.8 8.7 %all-gather = f32[8,128,128]{2,1,0:T(8,128)S(1)} all-gather(f32[4,128,128]{2,1,0:T(8,128)S(1)} %get-tuple-element.20), channel_id=2, replica_groups=mesh['seq_0'=4,'seq_1'=16,'seq_2'=2,'head'=4] {'seq_2'}, dimensions={0}, use_global_device_ids=true | all-gather | bytes 786432 | tf_op jit(solution)/shard_map/all_gather | solution.py:27
  18.5 0.8 copy-done
  19.3 0.7 slice_add_fusion.17
  20.0 0.0 all-gather.13.cloned.1.call-update
  20.0 0.0 all-gather.15.cloned.1.call-start
  20.1 0.0 copy-done.6
  20.1 0.1 copy.94
  20.2 0.2 copy.95
  20.4 1.4 fusion.71
  21.8 2.2 all-gather.1
  24.0 0.7 slice_add_fusion.8
  24.7 0.0 all-gather.15.cloned.1.call-update
  24.8 2.9 %copy.112 = bf16[512,2048]{0,1:T(8,128)(2,1)S(1)} copy(bf16[512,2048]{1,0:T(8,128)(2,1)} %param.9) | data formatting | bytes 4194304 | tf_op args[4]
  27.6 2.4 copy.113
  30.1 4.6 %all-to-all-start.1 = ((bf16[512,4,512]{2,0,1:T(8,128)(2,1)}), bf16[512,4,512]{2,0,1:T(8,128)(2,1)}, u32[]{:S(2)}, u32[]{:S(2)}) async-start(bf16[512,4,512]{2,0,1:T(8,128)(2,1)} %copy.113), calls=%async_computation.1 | async-start | bytes 4194304 | tf_op jit(solution)/shard_map/all_to_all | solution.py:139
  34.7 0.0 all-gather.9.cloned.1.call-start
  34.8 0.1 copy.79
  34.9 0.1 fusion.20
  35.0 54.6 %all-gather.13.cloned.1.call-done = f32[64,128,128]{2,1,0:T(8,128)} async-done(((f32[4,128,128]{2,1,0:T(8,128)}), f32[64,128,128]{2,1,0:T(8,128)}) %all-gather.13.cloned.1.call-update) | async-done | bytes 4194320 | tf_op jit(solution)/shard_map/all_gather | solution.py:27
  89.6 3.1 %bitcast_add_fusion.6 = (f32[1,4,128,128]{3,2,1,0:T(8,128)}, f32[1,4,128,128]{3,2,1,0:T(8,128)S(1)}, f32[4,128,128]{2,1,0:T(8,128)S(1)}) fusion(f32[64,128,128]{2,1,0:T(8,128)} %all-gather.13.cloned.1.call-done), kind=kLoop, calls=%fused_computation.125 | loop fusion | flops 983040 | bytes 4980736 | tf_op jit(solution)/shard_map/add | solution.py:65
  92.7 0.0 all-gather.9.cloned.1.call-update
  92.7 0.2 all-gather.11.cloned.1.call-start
  93.0 0.2 copy.80
  93.2 0.7 convolution_multiply_fusion.5
  93.9 0.7 convolution_multiply_fusion.2
  94.5 1.1 convolution_add_fusion.9
  95.6 1.1 convolution_add_fusion.4
  96.7 69.6 %all-gather.15.cloned.1.call-done = f32[64,128,128]{2,1,0:T(8,128)} async-done(((f32[4,128,128]{2,1,0:T(8,128)}), f32[64,128,128]{2,1,0:T(8,128)}) %all-gather.15.cloned.1.call-update) | async-done | bytes 4194320 | tf_op jit(solution)/shard_map/all_gather | solution.py:27
  166.3 3.1 %bitcast_add_fusion.1 = (f32[1,4,128,128]{3,2,1,0:T(8,128)}, f32[1,4,128,128]{3,2,1,0:T(8,128)S(1)}, f32[4,128,128]{2,1,0:T(8,128)S(1)}) fusion(f32[64,128,128]{2,1,0:T(8,128)} %all-gather.15.cloned.1.call-done), kind=kLoop, calls=%fused_computation.108 | loop fusion | flops 983040 | bytes 4980736 | tf_op jit(solution)/shard_map/add | solution.py:65
  169.4 0.0 all-gather.11.cloned.1.call-update
  169.4 35.2 %all-gather.9.cloned.1.call-done = f32[4,4,128,128]{3,2,1,0:T(8,128)} async-done(((f32[1,4,128,128]{3,2,1,0:T(8,128)}), f32[4,4,128,128]{3,2,1,0:T(8,128)}) %all-gather.9.cloned.1.call-update) | async-done | bytes 1048592 | tf_op jit(solution)/shard_map/all_gather | solution.py:27
  204.6 3.0 %fusion.37 = f32[4,128,128]{2,1,0:T(8,128)S(1)} fusion(f32[4,4,128,128]{3,2,1,0:T(8,128)} %all-gather.9.cloned.1.call-done, f32[1,4,128,128]{3,2,1,0:T(8,128)S(1)} %get-tuple-element.11, f32[4,128,128]{2,1,0:T(8,128)S(1)} %get-tuple-element.12, f32[64,128,128]{2,1,0:T(8,128)} %all-gather.13.cloned.1.call-done, f32[8,128,128]{2,1,0:T(8,128)S(1)} %copy-done.1, ...), kind=kLoop, calls=%fused_computation.70 | loop fusion | flops 2686976 | bytes 6029334 | tf_op jit(solution)/shard_map/add | solution.py:65
  207.6 0.6 multiply_reduce_fusion.4
  208.2 0.0 copy-done.2
  208.2 0.0 copy-done.4
  208.2 0.6 multiply_reduce_fusion.3
  208.8 0.4 multiply_add_fusion.3
  209.2 0.7 convolution_multiply_fusion.4
  209.9 0.4 convolution_add_fusion.7
  210.3 0.5 fusion.12
  210.8 0.2 multiply_add_fusion.1
  211.0 0.7 convolution_multiply_fusion.1
  211.7 0.4 convolution_add_fusion.2
  212.1 0.5 fusion.13
  212.6 26.0 %all-gather.11.cloned.1.call-done = f32[4,4,128,128]{3,2,1,0:T(8,128)} async-done(((f32[1,4,128,128]{3,2,1,0:T(8,128)}), f32[4,4,128,128]{3,2,1,0:T(8,128)}) %all-gather.11.cloned.1.call-update) | async-done | bytes 1048592 | tf_op jit(solution)/shard_map/all_gather | solution.py:27
  238.6 3.0 %fusion.27 = f32[4,128,128]{2,1,0:T(8,128)S(1)} fusion(f32[4,4,128,128]{3,2,1,0:T(8,128)} %all-gather.11.cloned.1.call-done, f32[1,4,128,128]{3,2,1,0:T(8,128)S(1)} %get-tuple-element.14, f32[4,128,128]{2,1,0:T(8,128)S(1)} %get-tuple-element.15, f32[64,128,128]{2,1,0:T(8,128)} %all-gather.15.cloned.1.call-done, f32[8,128,128]{2,1,0:T(8,128)S(1)} %all-gather.1, ...), kind=kLoop, calls=%fused_computation.45 | loop fusion | flops 2686976 | bytes 6029334 | tf_op jit(solution)/shard_map/add | solution.py:65
  241.6 0.8 convolution_multiply_fusion
  242.4 0.5 fusion.22
  242.9 0.3 fusion.11
  243.2 0.5 fusion.67
  243.7 0.8 convolution_multiply_fusion.3
  244.5 0.3 fusion.10
  244.8 0.1 copy.110
  244.9 0.1 copy.111
  245.1 0.0 all-to-all-done.1
  245.1 0.1 broadcast_in_dim.5
  245.2 17.0 %all_to_all.21 = bf16[4,256,512]{2,1,0:T(8,128)(2,1)S(1)} all-to-all(bf16[4,256,512]{2,1,0:T(8,128)(2,1)S(1)} %broadcast_in_dim.5), channel_id=1, replica_groups=mesh['seq_0'=4,'seq_1'=16,'seq_2'=2,'head'=4] {'head'}, dimensions={0} | all-to-all | bytes 2097152 | tf_op jit(solution)/shard_map/all_to_all | solution.py:39
  262.2 3.0 %fusion.5 = bf16[256,512]{1,0:T(8,128)(2,1)} fusion(bf16[512,4,512]{2,0,1:T(8,128)(2,1)} %all-to-all-done.1, bf16[4,256,512]{2,1,0:T(8,128)(2,1)S(1)} %all_to_all.21), kind=kOutput, calls=%fused_computation.3 | convolution fusion | flops 537001984 | bytes 3407872 | tf_op jit(solution)/shard_map/dot_general | solution.py:140
  (24 shorter events, 0.2 us)
Async XLA Ops:
  6.5 83.1 %all-gather.13.cloned.1.call-start = ((), (), s32[]{:S(2)}) async-start(), calls=%async_computation.4 | async-start | bytes 4456448 | tf_op jit(solution)/shard_map/all_gather | solution.py:27
  8.0 12.1 %copy-start.6 = (bf16[256,512]{1,0:T(8,128)(2,1)S(1)}, bf16[256,512]{1,0:T(8,128)(2,1)}, u32[]{:S(2)}) copy-start(bf16[256,512]{1,0:T(8,128)(2,1)} %param.7) | copy-start | bytes 786436
  18.5 0.8 copy-start
  20.0 146.3 %all-gather.15.cloned.1.call-start = ((), (), s32[]{:S(2)}) async-start(), calls=%async_computation.5 | async-start | bytes 4456448 | tf_op jit(solution)/shard_map/all_gather | solution.py:27
  30.1 4.7 %copy-start.7 = (bf16[256,512]{1,0:T(8,128)(2,1)S(1)}, bf16[256,512]{1,0:T(8,128)(2,1)}, u32[]{:S(2)}) copy-start(bf16[256,512]{1,0:T(8,128)(2,1)} %param.5) | copy-start | bytes 786436
  30.1 215.0 %all-to-all-start.1 = ((bf16[512,4,512]{2,0,1:T(8,128)(2,1)}), bf16[512,4,512]{2,0,1:T(8,128)(2,1)}, u32[]{:S(2)}, u32[]{:S(2)}) async-start(bf16[512,4,512]{2,0,1:T(8,128)(2,1)} %copy.113), calls=%async_computation.1 | async-start | bytes 4194304 | tf_op jit(solution)/shard_map/all_to_all | solution.py:139
  34.7 169.9 %all-gather.9.cloned.1.call-start = ((), (), s32[]{:S(2)}) async-start(), calls=%async_computation.2 | async-start | bytes 1310720 | tf_op jit(solution)/shard_map/all_gather | solution.py:27
  92.7 1.9 copy-start.8
  92.7 145.9 %all-gather.11.cloned.1.call-start = ((), (), s32[]{:S(2)}) async-start(), calls=%async_computation.3 | async-start | bytes 1310720 | tf_op jit(solution)/shard_map/all_gather | solution.py:27
  96.7 107.8 %copy-start.1 = (f32[8,128,128]{2,1,0:T(8,128)S(1)}, f32[8,128,128]{2,1,0:T(8,128)}, u32[]{:S(2)}) copy-start(f32[8,128,128]{2,1,0:T(8,128)} %copy-done) | copy-start | bytes 1572868
  204.6 3.0 %copy-start.5 = (f32[4,128,128]{2,1,0:T(8,128)S(1)}, f32[4,128,128]{2,1,0:T(8,128)}, u32[]{:S(2)}) copy-start(f32[4,128,128]{2,1,0:T(8,128)} %convolution_add_fusion.9) | copy-start | bytes 786436
  204.6 3.6 %copy-start.2 = (f32[4,2,128,128]{3,2,1,0:T(8,128)S(1)}, f32[4,2,128,128]{3,2,1,0:T(8,128)}, u32[]{:S(2)}) copy-start(f32[4,2,128,128]{3,2,1,0:T(8,128)} %get-tuple-element.21) | copy-start | bytes 1572868
  204.6 3.6 %copy-start.4 = (f32[4,128,128]{2,1,0:T(8,128)S(1)}, f32[4,128,128]{2,1,0:T(8,128)}, u32[]{:S(2)}) copy-start(f32[4,128,128]{2,1,0:T(8,128)} %convolution_add_fusion.4) | copy-start | bytes 786436
  238.6 3.8 %copy-start.3 = (f32[4,2,128,128]{3,2,1,0:T(8,128)S(1)}, f32[4,2,128,128]{3,2,1,0:T(8,128)}, u32[]{:S(2)}) copy-start(f32[4,2,128,128]{3,2,1,0:T(8,128)} %get-tuple-element.19) | copy-start | bytes 1572868
Sparse Core Ops, SparseCore 0:
  20.2 69.4 all-gather.12
  91.7 74.5 all-gather.14
  168.4 36.1 all-gather.8
  206.5 32.0 all-gather.10
where the time goes:
time: 273 us; the launch traced here: 272 us
  waiting for transfers between devices  185 us (68%)
  blocking collectives  27.9 us (10%)
  matrix products  17.2 us (6%)
  other arithmetic  14.5 us (5%)
  between operations  13.5 us (5%)
  local copies, waits for them, and re-layouts  8.35 us (3%)
  starting transfers between devices  4.93 us (2%)
    all_gather x4, waiting for transfers between devices, entering(): pieces = jax.tree.map(lambda part: lax.all_gather(part, axis), total)  185 us
    all_to_all x1, blocking collectives, copy_for_each(): lax.all_to_all(jnp.broadcast_to(value[None], (length, *value.shape)), axi...  17 us
    add x6, other arithmetic, add_states(): return (earlier[0] + later[0], earlier[1] + later[1])  13.6 us
    all_gather x2, blocking collectives, entering(): pieces = jax.tree.map(lambda part: lax.all_gather(part, axis), total)  10.8 us
  transfers between devices with their start and end apart: 5, of which 4 were waited for; matrix products, arithmetic and copies ran while one was open for 12% of the time, Pallas kernels for 0%

commit v1 on v0

v1 whole, which is shorter than its diff:
```python
import jax
import jax.numpy as jnp
from jax import lax
from jax.experimental import pallas as pl
from jax.experimental.pallas import tpu as pltpu
from jax.sharding import Mesh
from jax.sharding import PartitionSpec as P

HD = 128
ITERS = 2
SEQ = ("y", "far", "near", "core")
NEAR = ("y", "near", "core")
EPS = 1e-06
f32, bf16 = jnp.float32, jnp.bfloat16


def vmem():
    return pl.BlockSpec(memory_space=pltpu.VMEM)


def smem():
    return pl.BlockSpec(memory_space=pltpu.SMEM)


def params():
    return pltpu.CompilerParams(vmem_limit_bytes=32 * 1024 * 1024)


def halves(value):
    high = value.astype(bf16)
    return high, (value - high.astype(f32)).astype(bf16)


def pack(value):
    return (value * value * (value * jnp.abs(value))).astype(bf16)


def unpack(coded):
    coded = coded.astype(f32)
    root = jnp.sqrt(jnp.sqrt(jnp.abs(coded)))
    return jnp.where(coded < 0.0, -root, root)


def stacked(value):
    return jnp.concatenate(halves(value), axis=0)


def dot(left, right):
    return jnp.dot(left, right, preferred_element_type=f32)


def key_scale(keys):
    keys = keys.astype(f32)
    return lax.rsqrt(jnp.sum(keys * keys, axis=1, keepdims=True) + EPS)


def grams(k_ref, v_ref, out_ref):
    heads = k_ref.shape[1] // HD
    for h in range(heads):
        cols = slice(h * HD, (h + 1) * HD)
        keys, values = k_ref[:, cols], v_ref[:, cols]
        scale = key_scale(keys)
        kn = keys.astype(f32) * scale
        key_side = jnp.concatenate(halves(kn * scale), axis=1)
        value_side = jnp.concatenate(halves(kn), axis=1)
        key_gram = dot(keys.T, key_side)
        value_gram = dot(values.T, value_side)
        out_ref[h] = pack(key_gram[:, :HD] + key_gram[:, HD:])
        out_ref[heads + h] = pack(value_gram[:, :HD] + value_gram[:, HD:])


def group_totals(near_ref, out_ref):
    for y in range(near_ref.shape[0]):
        total = unpack(near_ref[y, 0])
        for member in range(1, near_ref.shape[1]):
            total += unpack(near_ref[y, member])
        total = pack(total)
        for far in range(out_ref.shape[0]):
            out_ref[far, y] = total


def prefixes(mine_ref, near_ref, far_ref, out_ref):
    mine = mine_ref[0]
    before = jnp.zeros(near_ref.shape[2:], f32)
    for y in range(near_ref.shape[0]):
        running = before
        for far in range(far_ref.shape[0]):
            total = unpack(far_ref[far, y])
            running += jnp.where(far < mine, total, 0.0)
            before += total
        for member in range(near_ref.shape[1]):
            out_ref[y, member] = pack(running)
            running += unpack(near_ref[y, member])


def solve(ridge_ref, q_ref, k_ref, v_ref, state_ref, w_ref, out_ref, mixed_ref):
    tokens, width = q_ref.shape
    heads = width // HD
    causal = lax.broadcasted_iota(jnp.int32, (tokens, tokens), 0) <= lax.broadcasted_iota(
        jnp.int32, (tokens, tokens), 1
    )
    for h in range(heads):
        cols = slice(h * HD, (h + 1) * HD)
        keys, values = k_ref[:, cols], v_ref[:, cols]
        scale = key_scale(keys)
        weight_k = jnp.where(causal, scale * scale, 0.0)
        weight_v = jnp.where(causal, scale, 0.0)
        keys_t = keys.T
        key_state = halves(unpack(state_ref[h]))
        value_state = halves(unpack(state_ref[heads + h]))

        def apply(state, split, weight, payload):
            left = jnp.concatenate([keys, state[0]], axis=0)
            both = dot(jnp.concatenate([left] * (split.shape[0] // HD), axis=1), split)
            scores = stacked(both[:tokens] * weight)
            within = dot(jnp.concatenate([payload, payload], axis=1), scores)
            return both[tokens:] + dot(state[1], split[:HD]) + within

        raw = q_ref[:, cols].T
        raw_f = raw.astype(f32)
        q_scale = lax.rsqrt(jnp.sum(raw_f * raw_f, axis=0, keepdims=True) + EPS)
        residual = raw_f * q_scale
        direction = residual
        norm = jnp.sum(residual * residual, axis=0, keepdims=True)
        estimate = None
        for sweep in range(ITERS):
            if sweep == 0:
                applied = apply(key_state, raw, weight_k, keys_t) * q_scale
            else:
                applied = apply(key_state, stacked(direction), weight_k, keys_t)
            applied += ridge_ref[h] * direction
            step = norm / (jnp.sum(direction * applied, axis=0, keepdims=True) + EPS)
            estimate = step * direction if estimate is None else estimate + step * direction
            if sweep + 1 < ITERS:
                residual = residual - step * applied
                fresh = jnp.sum(residual * residual, axis=0, keepdims=True)
                direction = residual + fresh / (norm + EPS) * direction
                norm = fresh
        mixed = apply(value_state, stacked(estimate), weight_v, values.T)
        mixed_ref[:, cols] = mixed.T.astype(bf16)
    mixed = mixed_ref[...]
    piece = out_ref.shape[2]
    for n in range(out_ref.shape[0]):
        out_ref[n] = dot(mixed, w_ref[:, n * piece : (n + 1) * piece]).astype(bf16)


def shards(queries, keys, values, ridges, out_weight):
    heads = ridges.shape[0]
    tokens, width = queries.shape
    spread = lax.axis_size("head")
    rows, far = lax.axis_size("y"), lax.axis_size("far")
    members = lax.axis_size("near") * lax.axis_size("core")
    piece = 2 * heads * HD // (rows * members)

    own = pl.pallas_call(
        grams,
        out_shape=jax.ShapeDtypeStruct((2 * heads, HD, HD), bf16),
        in_specs=[vmem()] * 2,
        out_specs=vmem(),
        compiler_params=params(),
        name="grams",
    )(keys, values)
    near = lax.all_to_all(own.reshape(rows * members, piece, HD), NEAR, 0, 0, tiled=True)
    near = near.reshape(rows, members, piece, HD)
    totals = pl.pallas_call(
        group_totals,
        out_shape=jax.ShapeDtypeStruct((far, rows, piece, HD), bf16),
        in_specs=[vmem()],
        out_specs=vmem(),
        compiler_params=params(),
        name="group_totals",
    )(near)
    totals = lax.all_to_all(totals, "far", 0, 0, tiled=True)
    states = pl.pallas_call(
        prefixes,
        out_shape=jax.ShapeDtypeStruct((rows, members, piece, HD), bf16),
        in_specs=[smem(), vmem(), vmem()],
        out_specs=vmem(),
        compiler_params=params(),
        name="prefixes",
    )(lax.axis_index("far").astype(jnp.int32).reshape(1), near, totals)
    states = lax.all_to_all(states.reshape(rows * members, piece, HD), NEAR, 0, 0, tiled=True)
    states = states.reshape(2 * heads, HD, HD)
    partial = pl.pallas_call(
        solve,
        out_shape=jax.ShapeDtypeStruct((spread, tokens, out_weight.shape[1] // spread), bf16),
        in_specs=[smem()] + [vmem()] * 5,
        out_specs=vmem(),
        scratch_shapes=[pltpu.VMEM((tokens, width), bf16)],
        compiler_params=params(),
        name="solve",
    )(ridges, queries, keys, values, states, out_weight)
    partial = lax.all_to_all(partial, "head", 0, 0, tiled=True)
    total = partial[0].astype(f32)
    for n in range(1, spread):
        total += partial[n].astype(f32)
    return total.astype(bf16)


def solution(mesh):
    split = Mesh(mesh.devices.reshape(4, 4, 4, 2, mesh.shape["head"]), (*SEQ, "head"))
    placed = (P(SEQ, "head"), P(SEQ, "head"), P(SEQ, "head"), P("head"), P("head", None))
    return jax.shard_map(
        shards, mesh=split, in_specs=placed, out_specs=P(SEQ, "head"), check_vma=False
    )
```

time: 273 us -> 93.2 us (0.34)
  waiting for transfers between devices: 185 us -> 12.4 us
  blocking collectives: 27.9 us -> 58.3 us
  matrix products: 17.2 us -> 0 us
  other arithmetic: 14.5 us -> 0.84 us
  between operations: 13.5 us -> 0.05 us
  starting transfers between devices: 4.93 us -> 12.1 us
  Pallas kernels: 0 us -> 7.16 us
  local copies, waits for them, and re-layouts: 8.35 us -> 2.07 us
    all_gather x4 -> x0, waiting for transfers between devices: 185 us -> none  [entering(): pieces = jax.tree.map(lambda part: lax.all_gather(part, axis), total)]
    all_to_all x1 -> x3, blocking collectives: 17 us -> 58.3 us  [the longest x1 21.3 us: shards(): lax.all_to_all(own.reshape(rows * members, piece, HD), NEAR, 0, 0, tiled=...]
    dot_general x21 -> x0, matrix products: 17.2 us -> none  [the longest x6 4.21 us: within(): jnp.einsum('hck,hsk->hcs', inputs, keyrows, precision=highest) * causal]
    add x8 -> x1, other arithmetic: 14.2 us -> 0.84 us  [shards(): total += partial[n].astype(f32)]
    all_to_all x1, waiting for transfers between devices: 0.01 us -> 12.4 us  [shards(): totals = lax.all_to_all(totals, 'far', 0, 0, tiled=True)]
    all_gather x2 -> x0, blocking collectives: 10.8 us -> none  [entering(): pieces = jax.tree.map(lambda part: lax.all_gather(part, axis), total)]
    all_to_all x1, starting transfers between devices: 4.63 us -> 12.1 us  [shards(): totals = lax.all_to_all(totals, 'far', 0, 0, tiled=True)]
    pallas_call x0 -> x4, Pallas kernels: none -> 7.16 us  [the longest x1 5.05 us: shards(): pl.pallas_call(solve, out_shape=jax.ShapeDtypeStruct((spread, tokens, out...]
  transfers between devices with their start and end apart: 5 -> 1, of which waited for: 4 -> 1; matrix products, arithmetic and copies ran while one was open for 12% -> 0% of each run, Pallas kernels for 0% -> 0%
where the time goes in v1:
time: 93.2 us; the launch traced here: 92.9 us
  blocking collectives  58.3 us (63%)
  waiting for transfers between devices  12.4 us (13%)
  starting transfers between devices  12.1 us (13%)
  Pallas kernels  7.16 us (8%)
  local copies, waits for them, and re-layouts  2.07 us (2%)
    all_to_all x1, blocking collectives, shards(): lax.all_to_all(own.reshape(rows * members, piece, HD), NEAR, 0, 0, tiled=...  21.3 us
    all_to_all x1, blocking collectives, shards(): partial = lax.all_to_all(partial, 'head', 0, 0, tiled=True)  18.7 us
    all_to_all x1, blocking collectives, shards(): lax.all_to_all(states.reshape(rows * members, piece, HD), NEAR, 0, 0, til...  18.3 us
    all_to_all x1, waiting for transfers between devices, shards(): totals = lax.all_to_all(totals, 'far', 0, 0, tiled=True)  12.4 us
    all_to_all x1, starting transfers between devices, shards(): totals = lax.all_to_all(totals, 'far', 0, 0, tiled=True)  12.1 us
    pallas_call x1, Pallas kernels, shards(): pl.pallas_call(solve, out_shape=jax.ShapeDtypeStruct((spread, tokens, out...  5.05 us
    unnamed x14, local copies, waits for them, and re-layouts  2.07 us
  transfers between devices with their start and end apart: 1, of which 1 were waited for; matrix products, arithmetic and copies ran while one was open for 0% of the time, Pallas kernels for 0%

profile of v1, /device:TPU:1, one launch (start us, length us, event | category | flops | bytes accessed | tf_op | source)
XLA Modules:
  0.0 92.9 jit_solution(17492633114552289911)
XLA Ops:
  0.0 0.0 copy-start
  0.0 0.0 copy-start.1
  0.0 1.1 %copy-done.1 = bf16[256,512]{1,0:T(8,128)(2,1)S(1)} copy-done((bf16[256,512]{1,0:T(8,128)(2,1)S(1)}, bf16[256,512]{1,0:T(8,128)(2,1)}, u32[]{:S(2)}) %copy-start.1) | copy-done | bytes 262168
  1.1 0.0 copy-start.3
  1.1 0.9 %copy-done.3 = bf16[256,512]{1,0:T(8,128)(2,1)S(1)} copy-done((bf16[256,512]{1,0:T(8,128)(2,1)S(1)}, bf16[256,512]{1,0:T(8,128)(2,1)}, u32[]{:S(2)}) %copy-start.3) | copy-done | bytes 262168
  2.1 0.0 copy-start.2
  2.1 0.0 copy-start.4
  2.1 0.0 copy-start.5
  2.1 0.0 copy-start.6
  2.1 0.5 grams.1
  2.6 21.3 %all_to_all.20 = bf16[32,32,128]{2,1,0:T(8,128)(2,1)S(1)} all-to-all(bf16[32,32,128]{2,1,0:T(8,128)(2,1)S(1)} %bitcast.10), channel_id=1, replica_groups=mesh['y'=4,'far'=4,'near'=4,'core'=2,'head'=4] {'y','near','core'}, dimensions={0} | all-to-all | bytes 524288 | tf_op jit(solution)/shard_map/all_to_all | solution.py:163
  23.9 1.0 %group_totals.1 = bf16[4,4,32,128]{3,2,1,0:T(8,128)(2,1)} custom-call(bf16[4,8,32,128]{3,2,1,0:T(8,128)(2,1)S(1)} %bitcast.7), custom_call_target="tpu_custom_call" | custom-call | tf_op jit(solution)/shard_map/group_totals/pallas_call | solution.py:165
  24.9 12.1 %all-to-all-start.1 = ((bf16[4,4,32,128]{3,2,1,0:T(8,128)(2,1)}), bf16[4,4,32,128]{3,2,1,0:T(8,128)(2,1)S(1)}, u32[]{:S(2)}, u32[]{:S(2)}) async-start(bf16[4,4,32,128]{3,2,1,0:T(8,128)(2,1)} %group_totals.1), calls=%async_computation.1 | async-start | bytes 262144 | tf_op jit(solution)/shard_map/all_to_all | solution.py:173
  37.0 12.4 %all-to-all-done.1.far_ref = bf16[4,4,32,128]{3,2,1,0:T(8,128)(2,1)S(1)} async-done(((bf16[4,4,32,128]{3,2,1,0:T(8,128)(2,1)}), bf16[4,4,32,128]{3,2,1,0:T(8,128)(2,1)S(1)}, u32[]{:S(2)}, u32[]{:S(2)}) %all-to-all-start.1) | async-done | bytes 131104 | tf_op jit(solution)/shard_map/all_to_all | solution.py:173
  49.4 0.6 prefixes.1
  50.0 18.3 %all_to_all.21 = bf16[32,32,128]{2,1,0:T(8,128)(2,1)S(1)} all-to-all(bf16[32,32,128]{2,1,0:T(8,128)(2,1)S(1)} %bitcast.11), channel_id=1, replica_groups=mesh['y'=4,'far'=4,'near'=4,'core'=2,'head'=4] {'y','near','core'}, dimensions={0} | all-to-all | bytes 524288 | tf_op jit(solution)/shard_map/all_to_all | solution.py:182
  68.3 0.0 copy-done
  68.3 0.0 copy-done.2
  68.3 0.0 copy-done.4
  68.3 0.0 copy-done.5
  68.3 0.0 copy-done.6
  68.3 5.1 %solve.1 = bf16[4,256,512]{2,1,0:T(8,128)(2,1)S(1)} custom-call(f32[4]{0:T(128)S(1)} %copy-done.6, bf16[256,512]{1,0:T(8,128)(2,1)S(1)} %copy-done.5, bf16[256,512]{1,0:T(8,128)(2,1)S(1)} %copy-done.2, bf16[256,512]{1,0:T(8,128)(2,1)S(1)} %copy-done.4, bf16[8,128,128]{2,1,0:T(8,128)(2,1)S(1)} %bitcast.9, bf16[512,2048]{1,0:T(8,128)(2,1)S(1)} %copy-done), custom_call_target="tpu_custom_call" | custom-call | tf_op jit(solution)/shard_map/solve/pallas_call | solution.py:184
  73.4 18.7 %all_to_all.22 = bf16[4,256,512]{2,1,0:T(8,128)(2,1)S(1)} all-to-all(bf16[4,256,512]{2,1,0:T(8,128)(2,1)S(1)} %solve.1), channel_id=1, replica_groups=mesh['y'=4,'far'=4,'near'=4,'core'=2,'head'=4] {'head'}, dimensions={0} | all-to-all | bytes 2097152 | tf_op jit(solution)/shard_map/all_to_all | solution.py:193
  92.1 0.8 fusion
Async XLA Ops:
  0.0 68.3 %copy-start = (bf16[512,2048]{1,0:T(8,128)(2,1)S(1)}, bf16[512,2048]{1,0:T(8,128)(2,1)}, u32[]{:S(2)}) copy-start(bf16[512,2048]{1,0:T(8,128)(2,1)} %w_ref.1) | copy-start | bytes 6291460
  0.0 1.1 %copy-start.1 = (bf16[256,512]{1,0:T(8,128)(2,1)S(1)}, bf16[256,512]{1,0:T(8,128)(2,1)}, u32[]{:S(2)}) copy-start(bf16[256,512]{1,0:T(8,128)(2,1)} %k_ref.3) | copy-start | bytes 786436
  1.1 0.9 %copy-start.3 = (bf16[256,512]{1,0:T(8,128)(2,1)S(1)}, bf16[256,512]{1,0:T(8,128)(2,1)}, u32[]{:S(2)}) copy-start(bf16[256,512]{1,0:T(8,128)(2,1)} %v_ref.3) | copy-start | bytes 786436
  2.1 66.2 %copy-start.2 = (bf16[256,512]{1,0:T(8,128)(2,1)S(1)}, bf16[256,512]{1,0:T(8,128)(2,1)}, u32[]{:S(2)}) copy-start(bf16[256,512]{1,0:T(8,128)(2,1)} %k_ref.3) | copy-start | bytes 786436
  2.1 66.2 %copy-start.4 = (bf16[256,512]{1,0:T(8,128)(2,1)S(1)}, bf16[256,512]{1,0:T(8,128)(2,1)}, u32[]{:S(2)}) copy-start(bf16[256,512]{1,0:T(8,128)(2,1)} %v_ref.3) | copy-start | bytes 786436
  2.1 66.2 %copy-start.5 = (bf16[256,512]{1,0:T(8,128)(2,1)S(1)}, bf16[256,512]{1,0:T(8,128)(2,1)}, u32[]{:S(2)}) copy-start(bf16[256,512]{1,0:T(8,128)(2,1)} %q_ref.1) | copy-start | bytes 786436
  2.1 66.2 %copy-start.6 = (f32[4]{0:T(128)S(1)}, f32[4]{0:T(128)}, u32[]{:S(2)}) copy-start(f32[4]{0:T(128)} %ridge_ref.1) | copy-start | bytes 52
  24.9 24.5 %all-to-all-start.1 = ((bf16[4,4,32,128]{3,2,1,0:T(8,128)(2,1)}), bf16[4,4,32,128]{3,2,1,0:T(8,128)(2,1)S(1)}, u32[]{:S(2)}, u32[]{:S(2)}) async-start(bf16[4,4,32,128]{3,2,1,0:T(8,128)(2,1)} %group_totals.1), calls=%async_computation.1 | async-start | bytes 262144 | tf_op jit(solution)/shard_map/all_to_all | solution.py:173

commit v2 on v1

--- a/solution.py
+++ b/solution.py
@@ -7,7 +7,6 @@
 from jax.sharding import PartitionSpec as P
 
 HD = 128
-ITERS = 2
 SEQ = ("y", "far", "near", "core")
 NEAR = ("y", "near", "core")
 EPS = 1e-06
@@ -39,10 +38,6 @@
     coded = coded.astype(f32)
     root = jnp.sqrt(jnp.sqrt(jnp.abs(coded)))
     return jnp.where(coded < 0.0, -root, root)
-
-
-def stacked(value):
-    return jnp.concatenate(halves(value), axis=0)
 
 
 def dot(left, right):
@@ -79,8 +74,8 @@
             out_ref[far, y] = total
 
 
-def prefixes(mine_ref, near_ref, far_ref, out_ref):
-    mine = mine_ref[0]
+def prefixes(near_ref, far_ref, out_ref):
+    mine = lax.axis_index("far")
     before = jnp.zeros(near_ref.shape[2:], f32)
     for y in range(near_ref.shape[0]):
         running = before
@@ -95,49 +90,55 @@
 
 def solve(ridge_ref, q_ref, k_ref, v_ref, state_ref, w_ref, out_ref, mixed_ref):
     tokens, width = q_ref.shape
-    heads = width // HD
+    heads = range(width // HD)
+    cols = [slice(h * HD, (h + 1) * HD) for h in heads]
     causal = lax.broadcasted_iota(jnp.int32, (tokens, tokens), 0) <= lax.broadcasted_iota(
         jnp.int32, (tokens, tokens), 1
     )
-    for h in range(heads):
-        cols = slice(h * HD, (h + 1) * HD)
-        keys, values = k_ref[:, cols], v_ref[:, cols]
-        scale = key_scale(keys)
-        weight_k = jnp.where(causal, scale * scale, 0.0)
-        weight_v = jnp.where(causal, scale, 0.0)
-        keys_t = keys.T
-        key_state = halves(unpack(state_ref[h]))
-        value_state = halves(unpack(state_ref[heads + h]))
-
-        def apply(state, split, weight, payload):
-            left = jnp.concatenate([keys, state[0]], axis=0)
-            both = dot(jnp.concatenate([left] * (split.shape[0] // HD), axis=1), split)
-            scores = stacked(both[:tokens] * weight)
-            within = dot(jnp.concatenate([payload, payload], axis=1), scores)
-            return both[tokens:] + dot(state[1], split[:HD]) + within
-
-        raw = q_ref[:, cols].T
-        raw_f = raw.astype(f32)
-        q_scale = lax.rsqrt(jnp.sum(raw_f * raw_f, axis=0, keepdims=True) + EPS)
-        residual = raw_f * q_scale
-        direction = residual
-        norm = jnp.sum(residual * residual, axis=0, keepdims=True)
-        estimate = None
-        for sweep in range(ITERS):
-            if sweep == 0:
-                applied = apply(key_state, raw, weight_k, keys_t) * q_scale
-            else:
-                applied = apply(key_state, stacked(direction), weight_k, keys_t)
-            applied += ridge_ref[h] * direction
-            step = norm / (jnp.sum(direction * applied, axis=0, keepdims=True) + EPS)
-            estimate = step * direction if estimate is None else estimate + step * direction
-            if sweep + 1 < ITERS:
-                residual = residual - step * applied
-                fresh = jnp.sum(residual * residual, axis=0, keepdims=True)
-                direction = residual + fresh / (norm + EPS) * direction
-                norm = fresh
-        mixed = apply(value_state, stacked(estimate), weight_v, values.T)
-        mixed_ref[:, cols] = mixed.T.astype(bf16)
+
+    def total(left, right):
+        return jnp.sum(left * right, axis=0, keepdims=True)
+
+    def apply(keys, state, vectors, scale, payload):
+        left = jnp.concatenate([keys, state[0]], axis=0)
+        left = jnp.concatenate([left] * len(vectors), axis=1)
+        both = dot(left, jnp.concatenate(vectors, axis=0))
+        scores = jnp.where(causal, both[:tokens] * scale, 0.0).astype(bf16)
+        return both[tokens:] + dot(state[1], vectors[0]) + dot(payload, scores)
+
+    keys = [k_ref[:, c] for c in cols]
+    scales = [key_scale(k) for k in keys]
+    squares = [s * s for s in scales]
+    raw = [q_ref[:, c].T for c in cols]
+    keys_t = [k.T for k in keys]
+    values_t = [v_ref[:, c].T for c in cols]
+    states = [halves(unpack(state_ref[h])) for h in heads]
+    floats = [r.astype(f32) for r in raw]
+    q_scales = [lax.rsqrt(total(f, f) + EPS) for f in floats]
+    first = [f * s for f, s in zip(floats, q_scales)]
+    norms = [total(d, d) for d in first]
+    applied = [
+        apply(keys[h], states[h], (raw[h],), squares[h], keys_t[h]) * q_scales[h]
+        + ridge_ref[h] * first[h]
+        for h in heads
+    ]
+    steps = [norms[h] / (total(first[h], applied[h]) + EPS) for h in heads]
+    residuals = [first[h] - steps[h] * applied[h] for h in heads]
+    fresh = [total(r, r) for r in residuals]
+    second = [residuals[h] + fresh[h] / (norms[h] + EPS) * first[h] for h in heads]
+    applied = [
+        apply(keys[h], states[h], halves(second[h]), squares[h], keys_t[h])
+        + ridge_ref[h] * second[h]
+        for h in heads
+    ]
+    last = [fresh[h] / (total(second[h], applied[h]) + EPS) for h in heads]
+    estimates = [steps[h] * first[h] + last[h] * second[h] for h in heads]
+    states = [halves(unpack(state_ref[len(heads) + h])) for h in heads]
+    mixed = [
+        apply(keys[h], states[h], halves(estimates[h]), scales[h], values_t[h]) for h in heads
+    ]
+    for h in heads:
+        mixed_ref[:, cols[h]] = mixed[h].T.astype(bf16)
     mixed = mixed_ref[...]
     piece = out_ref.shape[2]
     for n in range(out_ref.shape[0]):
@@ -174,11 +175,11 @@
     states = pl.pallas_call(
         prefixes,
         out_shape=jax.ShapeDtypeStruct((rows, members, piece, HD), bf16),
-        in_specs=[smem(), vmem(), vmem()],
+        in_specs=[vmem(), vmem()],
         out_specs=vmem(),
         compiler_params=params(),
         name="prefixes",
-    )(lax.axis_index("far").astype(jnp.int32).reshape(1), near, totals)
+    )(near, totals)
     states = lax.all_to_all(states.reshape(rows * members, piece, HD), NEAR, 0, 0, tiled=True)
     states = states.reshape(2 * heads, HD, HD)
     partial = pl.pallas_call(

time: 93.2 us -> 90.3 us (0.969)
  blocking collectives: 58.3 us -> 82.6 us
  waiting for transfers between devices: 12.4 us -> 0 us
  starting transfers between devices: 12.1 us -> 0 us
  Pallas kernels: 7.16 us -> 4.55 us
    all_to_all x0 -> x1, blocking collectives: none -> 24.3 us  [shards(): totals = lax.all_to_all(totals, 'far', 0, 0, tiled=True)]
    all_to_all x1 -> x0, waiting for transfers between devices: 12.4 us -> none  [shards(): totals = lax.all_to_all(totals, 'far', 0, 0, tiled=True)]
    all_to_all x1 -> x0, starting transfers between devices: 12.1 us -> none  [shards(): totals = lax.all_to_all(totals, 'far', 0, 0, tiled=True)]
    pallas_call x1, Pallas kernels: 5.05 us -> 3.11 us  [shards(): pl.pallas_call(solve, out_shape=jax.ShapeDtypeStruct((spread, tokens, out...]
    unnamed x14 -> x12, local copies, waits for them, and re-layouts: 2.07 us -> 2.06 us
  transfers between devices with their start and end apart: 1 -> 0, of which waited for: 1 -> 0; matrix products, arithmetic and copies ran while one was open for 0% -> 0% of each run, Pallas kernels for 0% -> 0%
where the time goes in v2:
time: 90.3 us; the launch traced here: 90.1 us
  blocking collectives  82.6 us (91%)
  Pallas kernels  4.55 us (5%)
  local copies, waits for them, and re-layouts  2.06 us (2%)
    all_to_all x1, blocking collectives, shards(): totals = lax.all_to_all(totals, 'far', 0, 0, tiled=True)  24.3 us
    all_to_all x1, blocking collectives, shards(): lax.all_to_all(own.reshape(rows * members, piece, HD), NEAR, 0, 0, tiled=...  21.3 us
    all_to_all x1, blocking collectives, shards(): partial = lax.all_to_all(partial, 'head', 0, 0, tiled=True)  18.7 us
    all_to_all x1, blocking collectives, shards(): lax.all_to_all(states.reshape(rows * members, piece, HD), NEAR, 0, 0, til...  18.3 us
    pallas_call x1, Pallas kernels, shards(): pl.pallas_call(solve, out_shape=jax.ShapeDtypeStruct((spread, tokens, out...  3.11 us
    unnamed x12, local copies, waits for them, and re-layouts  2.06 us

profile of v2, /device:TPU:1, one launch (start us, length us, event | category | flops | bytes accessed | tf_op | source)
XLA Modules:
  0.0 90.1 jit_solution(18346947650576874563)
XLA Ops:
  0.0 0.0 copy-start
  0.0 0.0 copy-start.1
  0.0 1.1 %copy-done.1 = bf16[256,512]{1,0:T(8,128)(2,1)S(1)} copy-done((bf16[256,512]{1,0:T(8,128)(2,1)S(1)}, bf16[256,512]{1,0:T(8,128)(2,1)}, u32[]{:S(2)}) %copy-start.1) | copy-done | bytes 262168
  1.1 0.0 copy-start.2
  1.1 0.9 %copy-done.2 = bf16[256,512]{1,0:T(8,128)(2,1)S(1)} copy-done((bf16[256,512]{1,0:T(8,128)(2,1)S(1)}, bf16[256,512]{1,0:T(8,128)(2,1)}, u32[]{:S(2)}) %copy-start.2) | copy-done | bytes 262168
  2.1 0.0 copy-start.3
  2.1 0.0 copy-start.4
  2.1 0.0 copy-start.5
  2.1 0.5 grams.1
  2.6 21.3 %all_to_all.20 = bf16[32,32,128]{2,1,0:T(8,128)(2,1)S(1)} all-to-all(bf16[32,32,128]{2,1,0:T(8,128)(2,1)S(1)} %bitcast.9), channel_id=1, replica_groups=mesh['y'=4,'far'=4,'near'=4,'core'=2,'head'=4] {'y','near','core'}, dimensions={0} | all-to-all | bytes 524288 | tf_op jit(solution)/shard_map/all_to_all | solution.py:164
  23.9 0.4 group_totals.1
  24.2 24.3 %all_to_all.21.far_ref = bf16[4,4,32,128]{3,2,1,0:T(8,128)(2,1)S(1)} all-to-all(bf16[4,4,32,128]{3,2,1,0:T(8,128)(2,1)S(1)} %group_totals.1), channel_id=1, replica_groups=mesh['y'=4,'far'=4,'near'=4,'core'=2,'head'=4] {'far'}, dimensions={0} | all-to-all | bytes 262144 | tf_op jit(solution)/shard_map/all_to_all | solution.py:174
  48.5 0.6 prefixes.1
  49.1 18.3 %all_to_all.22 = bf16[32,32,128]{2,1,0:T(8,128)(2,1)S(1)} all-to-all(bf16[32,32,128]{2,1,0:T(8,128)(2,1)S(1)} %bitcast.10), channel_id=1, replica_groups=mesh['y'=4,'far'=4,'near'=4,'core'=2,'head'=4] {'y','near','core'}, dimensions={0} | all-to-all | bytes 524288 | tf_op jit(solution)/shard_map/all_to_all | solution.py:183
  67.4 0.0 copy-done
  67.4 0.0 copy-done.3
  67.4 0.0 copy-done.4
  67.4 0.0 copy-done.5
  67.4 3.1 %solve.1 = bf16[4,256,512]{2,1,0:T(8,128)(2,1)S(1)} custom-call(f32[4]{0:T(128)S(1)} %copy-done.5, bf16[256,512]{1,0:T(8,128)(2,1)S(1)} %copy-done.4, bf16[256,512]{1,0:T(8,128)(2,1)S(1)} %copy-done.1, bf16[256,512]{1,0:T(8,128)(2,1)S(1)} %copy-done.3, bf16[8,128,128]{2,1,0:T(8,128)(2,1)S(1)} %bitcast.8, bf16[512,2048]{1,0:T(8,128)(2,1)S(1)} %copy-done), custom_call_target="tpu_custom_call" | custom-call | tf_op jit(solution)/shard_map/solve/pallas_call | solution.py:185
  70.5 18.7 %all_to_all.23 = bf16[4,256,512]{2,1,0:T(8,128)(2,1)S(1)} all-to-all(bf16[4,256,512]{2,1,0:T(8,128)(2,1)S(1)} %solve.1), channel_id=1, replica_groups=mesh['y'=4,'far'=4,'near'=4,'core'=2,'head'=4] {'head'}, dimensions={0} | all-to-all | bytes 2097152 | tf_op jit(solution)/shard_map/all_to_all | solution.py:194
  89.2 0.8 fusion
Async XLA Ops:
  0.0 67.4 %copy-start = (bf16[512,2048]{1,0:T(8,128)(2,1)S(1)}, bf16[512,2048]{1,0:T(8,128)(2,1)}, u32[]{:S(2)}) copy-start(bf16[512,2048]{1,0:T(8,128)(2,1)} %w_ref.1) | copy-start | bytes 6291460
  0.0 1.1 %copy-start.1 = (bf16[256,512]{1,0:T(8,128)(2,1)S(1)}, bf16[256,512]{1,0:T(8,128)(2,1)}, u32[]{:S(2)}) copy-start(bf16[256,512]{1,0:T(8,128)(2,1)} %k_ref.3) | copy-start | bytes 786436
  1.1 0.9 %copy-start.2 = (bf16[256,512]{1,0:T(8,128)(2,1)S(1)}, bf16[256,512]{1,0:T(8,128)(2,1)}, u32[]{:S(2)}) copy-start(bf16[256,512]{1,0:T(8,128)(2,1)} %v_ref.3) | copy-start | bytes 786436
  2.1 65.3 %copy-start.3 = (bf16[256,512]{1,0:T(8,128)(2,1)S(1)}, bf16[256,512]{1,0:T(8,128)(2,1)}, u32[]{:S(2)}) copy-start(bf16[256,512]{1,0:T(8,128)(2,1)} %v_ref.3) | copy-start | bytes 786436
  2.1 65.3 %copy-start.4 = (bf16[256,512]{1,0:T(8,128)(2,1)S(1)}, bf16[256,512]{1,0:T(8,128)(2,1)}, u32[]{:S(2)}) copy-start(bf16[256,512]{1,0:T(8,128)(2,1)} %q_ref.1) | copy-start | bytes 786436
  2.1 65.3 %copy-start.5 = (f32[4]{0:T(128)S(1)}, f32[4]{0:T(128)}, u32[]{:S(2)}) copy-start(f32[4]{0:T(128)} %ridge_ref.1) | copy-start | bytes 52

commit v3 on v2

--- a/solution.py
+++ b/solution.py
@@ -23,6 +23,14 @@
 
 def params():
     return pltpu.CompilerParams(vmem_limit_bytes=32 * 1024 * 1024)
+
+
+def far_groups():
+    return [[near + 4 * far if far < 2 else (near + 2) % 4 + 4 * far for far in range(4)] for near in range(4)]
+
+
+def turned(matrix):
+    return matrix ^ (lax.axis_index("far") // 2)
 
 
 def halves(value):
@@ -60,8 +68,8 @@
         value_side = jnp.concatenate(halves(kn), axis=1)
         key_gram = dot(keys.T, key_side)
         value_gram = dot(values.T, value_side)
-        out_ref[h] = pack(key_gram[:, :HD] + key_gram[:, HD:])
-        out_ref[heads + h] = pack(value_gram[:, :HD] + value_gram[:, HD:])
+        out_ref[turned(h)] = pack(key_gram[:, :HD] + key_gram[:, HD:])
+        out_ref[turned(heads + h)] = pack(value_gram[:, :HD] + value_gram[:, HD:])
 
 
 def group_totals(near_ref, out_ref):
@@ -112,7 +120,7 @@
     raw = [q_ref[:, c].T for c in cols]
     keys_t = [k.T for k in keys]
     values_t = [v_ref[:, c].T for c in cols]
-    states = [halves(unpack(state_ref[h])) for h in heads]
+    states = [halves(unpack(state_ref[turned(h)])) for h in heads]
     floats = [r.astype(f32) for r in raw]
     q_scales = [lax.rsqrt(total(f, f) + EPS) for f in floats]
     first = [f * s for f, s in zip(floats, q_scales)]
@@ -133,7 +141,7 @@
     ]
     last = [fresh[h] / (total(second[h], applied[h]) + EPS) for h in heads]
     estimates = [steps[h] * first[h] + last[h] * second[h] for h in heads]
-    states = [halves(unpack(state_ref[len(heads) + h])) for h in heads]
+    states = [halves(unpack(state_ref[turned(len(heads) + h)])) for h in heads]
     mixed = [
         apply(keys[h], states[h], halves(estimates[h]), scales[h], values_t[h]) for h in heads
     ]
@@ -171,7 +179,9 @@
         compiler_params=params(),
         name="group_totals",
     )(near)
-    totals = lax.all_to_all(totals, "far", 0, 0, tiled=True)
+    totals = lax.all_to_all(
+        totals, ("far", "near"), 0, 0, axis_index_groups=far_groups(), tiled=True
+    )
     states = pl.pallas_call(
         prefixes,
         out_shape=jax.ShapeDtypeStruct((rows, members, piece, HD), bf16),

time: 90.3 us -> 87.8 us (0.972)
  blocking collectives: 82.6 us -> 80.1 us
    all_to_all x1, blocking collectives: 24.3 us -> 20.7 us  [shards(): lax.all_to_all(totals, ('far', 'near'), 0, 0, axis_index_groups=far_group...]
    all_to_all x1, blocking collectives: 18.3 us -> 19.4 us  [shards(): lax.all_to_all(states.reshape(rows * members, piece, HD), NEAR, 0, 0, til...]
where the time goes in v3:
time: 87.8 us; the launch traced here: 87.5 us
  blocking collectives  80.1 us (91%)
  Pallas kernels  4.51 us (5%)
  local copies, waits for them, and re-layouts  2.06 us (2%)
    all_to_all x1, blocking collectives, shards(): lax.all_to_all(own.reshape(rows * members, piece, HD), NEAR, 0, 0, tiled=...  21.3 us
    all_to_all x1, blocking collectives, shards(): lax.all_to_all(totals, ('far', 'near'), 0, 0, axis_index_groups=far_group...  20.7 us
    all_to_all x1, blocking collectives, shards(): lax.all_to_all(states.reshape(rows * members, piece, HD), NEAR, 0, 0, til...  19.4 us
    all_to_all x1, blocking collectives, shards(): partial = lax.all_to_all(partial, 'head', 0, 0, tiled=True)  18.7 us
    pallas_call x1, Pallas kernels, shards(): pl.pallas_call(solve, out_shape=jax.ShapeDtypeStruct((spread, tokens, out...  3.08 us
    unnamed x12, local copies, waits for them, and re-layouts  2.06 us

profile of v3, /device:TPU:1, one launch (start us, length us, event | category | flops | bytes accessed | tf_op | source)
XLA Modules:
  0.0 87.5 jit_solution(8878408430355397633)
XLA Ops:
  0.0 0.0 copy-start
  0.0 0.0 copy-start.1
  0.0 1.1 %copy-done.1 = bf16[256,512]{1,0:T(8,128)(2,1)S(1)} copy-done((bf16[256,512]{1,0:T(8,128)(2,1)S(1)}, bf16[256,512]{1,0:T(8,128)(2,1)}, u32[]{:S(2)}) %copy-start.1) | copy-done | bytes 262168
  1.1 0.0 copy-start.2
  1.1 0.9 %copy-done.2 = bf16[256,512]{1,0:T(8,128)(2,1)S(1)} copy-done((bf16[256,512]{1,0:T(8,128)(2,1)S(1)}, bf16[256,512]{1,0:T(8,128)(2,1)}, u32[]{:S(2)}) %copy-start.2) | copy-done | bytes 262168
  2.1 0.0 copy-start.3
  2.1 0.0 copy-start.4
  2.1 0.0 copy-start.5
  2.1 0.5 grams.1
  2.6 21.3 %all_to_all.20 = bf16[32,32,128]{2,1,0:T(8,128)(2,1)S(1)} all-to-all(bf16[32,32,128]{2,1,0:T(8,128)(2,1)S(1)} %bitcast.9), channel_id=1, replica_groups=mesh['y'=4,'far'=4,'near'=4,'core'=2,'head'=4] {'y','near','core'}, dimensions={0} | all-to-all | bytes 524288 | tf_op jit(solution)/shard_map/all_to_all | solution.py:172
  23.8 0.4 group_totals.1
  24.2 20.7 %all_to_all.21.far_ref = bf16[4,4,32,128]{3,2,1,0:T(8,128)(2,1)S(1)} all-to-all(bf16[4,4,32,128]{3,2,1,0:T(8,128)(2,1)S(1)} %group_totals.1), channel_id=1, replica_groups={{0,32,80,112},{8,40,88,120},{16,48,64,96},{24,56,72,104},{1,33,81,113},..., dimensions={0} | all-to-all | bytes 262144 | tf_op jit(solution)/shard_map/all_to_all | solution.py:182
  44.8 0.6 prefixes.1
  45.4 19.4 %all_to_all.22 = bf16[32,32,128]{2,1,0:T(8,128)(2,1)S(1)} all-to-all(bf16[32,32,128]{2,1,0:T(8,128)(2,1)S(1)} %bitcast.10), channel_id=1, replica_groups=mesh['y'=4,'far'=4,'near'=4,'core'=2,'head'=4] {'y','near','core'}, dimensions={0} | all-to-all | bytes 524288 | tf_op jit(solution)/shard_map/all_to_all | solution.py:193
  64.8 0.0 copy-done
  64.8 0.0 copy-done.3
  64.8 0.0 copy-done.4
  64.9 0.0 copy-done.5
  64.9 3.1 %solve.1 = bf16[4,256,512]{2,1,0:T(8,128)(2,1)S(1)} custom-call(f32[4]{0:T(128)S(1)} %copy-done.5, bf16[256,512]{1,0:T(8,128)(2,1)S(1)} %copy-done.4, bf16[256,512]{1,0:T(8,128)(2,1)S(1)} %copy-done.1, bf16[256,512]{1,0:T(8,128)(2,1)S(1)} %copy-done.3, bf16[8,128,128]{2,1,0:T(8,128)(2,1)S(1)} %bitcast.8, bf16[512,2048]{1,0:T(8,128)(2,1)S(1)} %copy-done), custom_call_target="tpu_custom_call" | custom-call | tf_op jit(solution)/shard_map/solve/pallas_call | solution.py:195
  68.0 18.7 %all_to_all.23 = bf16[4,256,512]{2,1,0:T(8,128)(2,1)S(1)} all-to-all(bf16[4,256,512]{2,1,0:T(8,128)(2,1)S(1)} %solve.1), channel_id=1, replica_groups=mesh['y'=4,'far'=4,'near'=4,'core'=2,'head'=4] {'head'}, dimensions={0} | all-to-all | bytes 2097152 | tf_op jit(solution)/shard_map/all_to_all | solution.py:204
  86.7 0.8 fusion
Async XLA Ops:
  0.0 64.8 %copy-start = (bf16[512,2048]{1,0:T(8,128)(2,1)S(1)}, bf16[512,2048]{1,0:T(8,128)(2,1)}, u32[]{:S(2)}) copy-start(bf16[512,2048]{1,0:T(8,128)(2,1)} %w_ref.1) | copy-start | bytes 6291460
  0.0 1.1 %copy-start.1 = (bf16[256,512]{1,0:T(8,128)(2,1)S(1)}, bf16[256,512]{1,0:T(8,128)(2,1)}, u32[]{:S(2)}) copy-start(bf16[256,512]{1,0:T(8,128)(2,1)} %k_ref.3) | copy-start | bytes 786436
  1.1 0.9 %copy-start.2 = (bf16[256,512]{1,0:T(8,128)(2,1)S(1)}, bf16[256,512]{1,0:T(8,128)(2,1)}, u32[]{:S(2)}) copy-start(bf16[256,512]{1,0:T(8,128)(2,1)} %v_ref.3) | copy-start | bytes 786436
  2.1 62.8 %copy-start.3 = (bf16[256,512]{1,0:T(8,128)(2,1)S(1)}, bf16[256,512]{1,0:T(8,128)(2,1)}, u32[]{:S(2)}) copy-start(bf16[256,512]{1,0:T(8,128)(2,1)} %v_ref.3) | copy-start | bytes 786436
  2.1 62.8 %copy-start.4 = (bf16[256,512]{1,0:T(8,128)(2,1)S(1)}, bf16[256,512]{1,0:T(8,128)(2,1)}, u32[]{:S(2)}) copy-start(bf16[256,512]{1,0:T(8,128)(2,1)} %q_ref.1) | copy-start | bytes 786436
  2.1 62.8 %copy-start.5 = (f32[4]{0:T(128)S(1)}, f32[4]{0:T(128)}, u32[]{:S(2)}) copy-start(f32[4]{0:T(128)} %ridge_ref.1) | copy-start | bytes 52

commit v4 on v3

--- a/solution.py
+++ b/solution.py
@@ -10,6 +10,7 @@
 SEQ = ("y", "far", "near", "core")
 NEAR = ("y", "near", "core")
 EPS = 1e-06
+ROWS = 4
 f32, bf16 = jnp.float32, jnp.bfloat16
 
 
@@ -29,8 +30,17 @@
     return [[near + 4 * far if far < 2 else (near + 2) % 4 + 4 * far for far in range(4)] for near in range(4)]
 
 
-def turned(matrix):
-    return matrix ^ (lax.axis_index("far") // 2)
+def turned(rows, turns):
+    size = rows.shape[0] // (2 * turns)
+    parts = [rows[n * size : (n + 1) * size] for n in range(2 * turns)]
+    upper = lax.axis_index("far") >= 2
+    return jnp.concatenate(
+        [jnp.where(upper, parts[n ^ 1], parts[n]) for n in range(2 * turns)], axis=0
+    )
+
+
+def position(axis):
+    return lax.broadcasted_iota(jnp.int32, (HD, HD), axis)
 
 
 def halves(value):
@@ -57,8 +67,9 @@
     return lax.rsqrt(jnp.sum(keys * keys, axis=1, keepdims=True) + EPS)
 
 
-def grams(k_ref, v_ref, out_ref):
+def grams(k_ref, v_ref, out_ref, rows_ref):
     heads = k_ref.shape[1] // HD
+    squares = []
     for h in range(heads):
         cols = slice(h * HD, (h + 1) * HD)
         keys, values = k_ref[:, cols], v_ref[:, cols]
@@ -68,35 +79,58 @@
         value_side = jnp.concatenate(halves(kn), axis=1)
         key_gram = dot(keys.T, key_side)
         value_gram = dot(values.T, value_side)
-        out_ref[turned(h)] = pack(key_gram[:, :HD] + key_gram[:, HD:])
-        out_ref[turned(heads + h)] = pack(value_gram[:, :HD] + value_gram[:, HD:])
-
-
-def group_totals(near_ref, out_ref):
-    for y in range(near_ref.shape[0]):
-        total = unpack(near_ref[y, 0])
-        for member in range(1, near_ref.shape[1]):
-            total += unpack(near_ref[y, member])
-        total = pack(total)
-        for far in range(out_ref.shape[0]):
-            out_ref[far, y] = total
-
-
-def prefixes(near_ref, far_ref, out_ref):
+        squares.append(key_gram[:, :HD] + key_gram[:, HD:])
+        rows_ref[h * HD : (h + 1) * HD] = value_gram[:, :HD] + value_gram[:, HD:]
+    tail = (heads + heads // 2) * HD
+    rows_ref[tail:] = jnp.zeros((rows_ref.shape[0] - tail, HD), f32)
+    for n in range(heads // 2):
+        one, other = squares[2 * n], squares[2 * n + 1]
+        at = (heads + n) * HD
+        rows_ref[at : at + HD] = jnp.where(position(0) <= position(1), one, other)
+        rows_ref[tail + n : tail + n + 1] = jnp.sum(
+            jnp.where(position(0) == position(1), other, 0.0), axis=0, keepdims=True
+        )
+    out_ref[...] = pack(turned(rows_ref[...], ROWS))
+
+
+def group_totals(near_ref, out_ref, terms_ref, total_ref):
+    terms_ref[...] = unpack(near_ref[...])
+    piece = total_ref.shape[0] // ROWS
+    members = near_ref.shape[0] // total_ref.shape[0]
+    for y in range(ROWS):
+        at = y * members * piece
+        total = terms_ref[at : at + piece]
+        for member in range(1, members):
+            total += terms_ref[at + member * piece : at + (member + 1) * piece]
+        total_ref[y * piece : (y + 1) * piece] = total
+    total = pack(total_ref[...])
+    for far in range(out_ref.shape[0]):
+        out_ref[far] = total
+
+
+def prefixes(terms_ref, far_ref, out_ref, total_ref, rows_ref):
     mine = lax.axis_index("far")
-    before = jnp.zeros(near_ref.shape[2:], f32)
-    for y in range(near_ref.shape[0]):
+    quarters, rows = far_ref.shape[:2]
+    piece = rows // ROWS
+    members = terms_ref.shape[0] // rows
+    for far in range(quarters):
+        total_ref[far * rows : (far + 1) * rows] = unpack(far_ref[far])
+    before = jnp.zeros((piece, HD), f32)
+    for y in range(ROWS):
         running = before
-        for far in range(far_ref.shape[0]):
-            total = unpack(far_ref[far, y])
+        for far in range(quarters):
+            at = far * rows + y * piece
+            total = total_ref[at : at + piece]
             running += jnp.where(far < mine, total, 0.0)
             before += total
-        for member in range(near_ref.shape[1]):
-            out_ref[y, member] = pack(running)
-            running += unpack(near_ref[y, member])
-
-
-def solve(ridge_ref, q_ref, k_ref, v_ref, state_ref, w_ref, out_ref, mixed_ref):
+        for member in range(members):
+            at = (y * members + member) * piece
+            rows_ref[at : at + piece] = running
+            running += terms_ref[at : at + piece]
+    out_ref[...] = pack(rows_ref[...])
+
+
+def solve(ridge_ref, q_ref, k_ref, v_ref, state_ref, w_ref, out_ref, mixed_ref, rows_ref):
     tokens, width = q_ref.shape
     heads = range(width // HD)
     cols = [slice(h * HD, (h + 1) * HD) for h in heads]
@@ -120,7 +154,17 @@
     raw = [q_ref[:, c].T for c in cols]
     keys_t = [k.T for k in keys]
     values_t = [v_ref[:, c].T for c in cols]
-    states = [halves(unpack(state_ref[turned(h)])) for h in heads]
+    rows_ref[...] = turned(unpack(state_ref[...]), ROWS)
+    upper, diagonal = position(0) <= position(1), position(0) == position(1)
+    tail = (len(heads) + len(heads) // 2) * HD
+    states = []
+    for n in range(len(heads) // 2):
+        at = (len(heads) + n) * HD
+        both = rows_ref[at : at + HD]
+        mirrored = both.T
+        states.append(halves(jnp.where(upper, both, mirrored)))
+        other = jnp.where(upper, mirrored, both)
+        states.append(halves(jnp.where(diagonal, rows_ref[tail + n : tail + n + 1], other)))
     floats = [r.astype(f32) for r in raw]
     q_scales = [lax.rsqrt(total(f, f) + EPS) for f in floats]
     first = [f * s for f, s in zip(floats, q_scales)]
@@ -141,7 +185,7 @@
     ]
     last = [fresh[h] / (total(second[h], applied[h]) + EPS) for h in heads]
     estimates = [steps[h] * first[h] + last[h] * second[h] for h in heads]
-    states = [halves(unpack(state_ref[turned(len(heads) + h)])) for h in heads]
+    states = [halves(rows_ref[h * HD : (h + 1) * HD]) for h in heads]
     mixed = [
         apply(keys[h], states[h], halves(estimates[h]), scales[h], values_t[h]) for h in heads
     ]
@@ -156,51 +200,60 @@
 def shards(queries, keys, values, ridges, out_weight):
     heads = ridges.shape[0]
     tokens, width = queries.shape
-    spread = lax.axis_size("head")
-    rows, far = lax.axis_size("y"), lax.axis_size("far")
-    members = lax.axis_size("near") * lax.axis_size("core")
-    piece = 2 * heads * HD // (rows * members)
-
+    spread, quarters = lax.axis_size("head"), lax.axis_size("far")
+    holders = ROWS * lax.axis_size("near") * lax.axis_size("core")
+    piece = 2 * pl.cdiv((heads + heads // 2) * HD + heads // 2, 2 * holders)
+
+    def exchange(rows):
+        rows = rows.reshape(holders, piece // 2, 2, HD)
+        return lax.all_to_all(rows, NEAR, 0, 0, tiled=True).reshape(holders * piece, HD)
+
+    def scratch(count):
+        return pltpu.VMEM((count * piece, HD), f32)
+
+    rows = jax.ShapeDtypeStruct((holders * piece, HD), bf16)
     own = pl.pallas_call(
         grams,
-        out_shape=jax.ShapeDtypeStruct((2 * heads, HD, HD), bf16),
+        out_shape=rows,
         in_specs=[vmem()] * 2,
         out_specs=vmem(),
+        scratch_shapes=[scratch(holders)],
         compiler_params=params(),
         name="grams",
     )(keys, values)
-    near = lax.all_to_all(own.reshape(rows * members, piece, HD), NEAR, 0, 0, tiled=True)
-    near = near.reshape(rows, members, piece, HD)
-    totals = pl.pallas_call(
+    totals, terms = pl.pallas_call(
         group_totals,
-        out_shape=jax.ShapeDtypeStruct((far, rows, piece, HD), bf16),
+        out_shape=(
+            jax.ShapeDtypeStruct((quarters, ROWS * piece, HD), bf16),
+            jax.ShapeDtypeStruct(rows.shape, f32),
+        ),
         in_specs=[vmem()],
-        out_specs=vmem(),
+        out_specs=(vmem(), vmem()),
+        scratch_shapes=[scratch(ROWS)],
         compiler_params=params(),
         name="group_totals",
-    )(near)
+    )(exchange(own))
     totals = lax.all_to_all(
         totals, ("far", "near"), 0, 0, axis_index_groups=far_groups(), tiled=True
     )
     states = pl.pallas_call(
         prefixes,
-        out_shape=jax.ShapeDtypeStruct((rows, members, piece, HD), bf16),
+        out_shape=rows,
         in_specs=[vmem(), vmem()],
         out_specs=vmem(),
+        scratch_shapes=[scratch(quarters * ROWS), scratch(holders)],
         compiler_params=params(),
         name="prefixes",
-    )(near, totals)
-    states = lax.all_to_all(states.reshape(rows * members, piece, HD), NEAR, 0, 0, tiled=True)
-    states = states.reshape(2 * heads, HD, HD)
+    )(terms, totals)
     partial = pl.pallas_call(
         solve,
         out_shape=jax.ShapeDtypeStruct((spread, tokens, out_weight.shape[1] // spread), bf16),
         in_specs=[smem()] + [vmem()] * 5,
         out_specs=vmem(),
-        scratch_shapes=[pltpu.VMEM((tokens, width), bf16)],
+        scratch_shapes=[pltpu.VMEM((tokens, width), bf16), scratch(holders)],
         compiler_params=params(),
         name="solve",
-    )(ridges, queries, keys, values, states, out_weight)
+    )(ridges, queries, keys, values, exchange(states), out_weight)
     partial = lax.all_to_all(partial, "head", 0, 0, tiled=True)
     total = partial[0].astype(f32)
     for n in range(1, spread):
@@ -209,7 +262,7 @@
 
 
 def solution(mesh):
-    split = Mesh(mesh.devices.reshape(4, 4, 4, 2, mesh.shape["head"]), (*SEQ, "head"))
+    split = Mesh(mesh.devices.reshape(ROWS, 4, 4, 2, mesh.shape["head"]), (*SEQ, "head"))
     placed = (P(SEQ, "head"), P(SEQ, "head"), P(SEQ, "head"), P("head"), P("head", None))
     return jax.shard_map(
         shards, mesh=split, in_specs=placed, out_specs=P(SEQ, "head"), check_vma=False

time: 87.8 us -> 85.8 us (0.977)
  blocking collectives: 80.1 us -> 77.3 us
  local copies, waits for them, and re-layouts: 2.06 us -> 3.01 us
    all_to_all x2, blocking collectives: 40.7 us -> 38.5 us  [exchange(): lax.all_to_all(rows, NEAR, 0, 0, tiled=True).reshape(holders * piece, HD)]
    unnamed x12 -> x14, local copies, waits for them, and re-layouts: 2.06 us -> 3.01 us
where the time goes in v4:
time: 85.8 us; the launch traced here: 85.5 us
  blocking collectives  77.3 us (90%)
  Pallas kernels  4.29 us (5%)
  local copies, waits for them, and re-layouts  3.01 us (4%)
    all_to_all x2, blocking collectives, exchange(): lax.all_to_all(rows, NEAR, 0, 0, tiled=True).reshape(holders * piece, HD)  38.5 us
    all_to_all x1, blocking collectives, shards(): lax.all_to_all(totals, ('far', 'near'), 0, 0, axis_index_groups=far_group...  20.2 us
    all_to_all x1, blocking collectives, shards(): partial = lax.all_to_all(partial, 'head', 0, 0, tiled=True)  18.6 us
    pallas_call x1, Pallas kernels, shards(): pl.pallas_call(solve, out_shape=jax.ShapeDtypeStruct((spread, tokens, out...  3.12 us
    unnamed x14, local copies, waits for them, and re-layouts  3.01 us

profile of v4, /device:TPU:1, one launch (start us, length us, event | category | flops | bytes accessed | tf_op | source)
XLA Modules:
  0.0 85.5 jit_solution(5926650411448861508)
XLA Ops:
  0.0 0.0 copy-start
  0.0 0.0 copy-start.1
  0.0 1.1 %copy-done.1 = bf16[256,512]{1,0:T(8,128)(2,1)S(1)} copy-done((bf16[256,512]{1,0:T(8,128)(2,1)S(1)}, bf16[256,512]{1,0:T(8,128)(2,1)}, u32[]{:S(2)}) %copy-start.1) | copy-done | bytes 262168
  1.1 0.0 copy-start.3
  1.1 0.9 %copy-done.3 = bf16[256,512]{1,0:T(8,128)(2,1)S(1)} copy-done((bf16[256,512]{1,0:T(8,128)(2,1)S(1)}, bf16[256,512]{1,0:T(8,128)(2,1)}, u32[]{:S(2)}) %copy-start.3) | copy-done | bytes 262168
  2.1 0.0 copy-start.2
  2.1 0.0 copy-start.4
  2.1 0.0 copy-start.6
  2.1 0.5 grams.1
  2.6 20.2 %all_to_all.20 = bf16[32,13,2,128]{3,2,1,0:T(2,128)(2,1)S(1)} all-to-all(bf16[32,13,2,128]{3,2,1,0:T(2,128)(2,1)S(1)} %bitcast.8), channel_id=1, replica_groups=mesh['y'=4,'far'=4,'near'=4,'core'=2,'head'=4] {'y','near','core'}, dimensions={0} | all-to-all | bytes 425984 | tf_op jit(solution)/shard_map/all_to_all | solution.py:209
  22.8 0.3 group_totals.1
  23.2 20.2 %all_to_all.21.far_ref = bf16[4,104,128]{2,1,0:T(8,128)(2,1)S(1)} all-to-all(bf16[4,104,128]{2,1,0:T(8,128)(2,1)S(1)} %get-tuple-element.8), channel_id=1, replica_groups={{0,32,80,112},{8,40,88,120},{16,48,64,96},{24,56,72,104},{1,33,81,113},..., dimensions={0} | all-to-all | bytes 212992 | tf_op jit(solution)/shard_map/all_to_all | solution.py:236
  43.3 0.3 prefixes.1
  43.6 18.3 %all_to_all.22 = bf16[32,13,2,128]{3,2,1,0:T(2,128)(2,1)S(1)} all-to-all(bf16[32,13,2,128]{3,2,1,0:T(2,128)(2,1)S(1)} %bitcast.7), channel_id=1, replica_groups=mesh['y'=4,'far'=4,'near'=4,'core'=2,'head'=4] {'y','near','core'}, dimensions={0} | all-to-all | bytes 425984 | tf_op jit(solution)/shard_map/all_to_all | solution.py:209
  61.9 0.0 copy-done
  61.9 0.0 copy-done.2
  61.9 0.0 copy-done.4
  61.9 0.0 copy-done.6
  61.9 0.0 copy-start.5
  61.9 0.9 %copy-done.5 = bf16[256,512]{1,0:T(8,128)(2,1)S(1)} copy-done((bf16[256,512]{1,0:T(8,128)(2,1)S(1)}, bf16[256,512]{1,0:T(8,128)(2,1)}, u32[]{:S(2)}) %copy-start.5) | copy-done | bytes 262168
  62.9 3.1 %solve.1 = bf16[4,256,512]{2,1,0:T(8,128)(2,1)S(1)} custom-call(f32[4]{0:T(128)S(1)} %copy-done.6, bf16[256,512]{1,0:T(8,128)(2,1)S(1)} %copy-done.5, bf16[256,512]{1,0:T(8,128)(2,1)S(1)} %copy-done.2, bf16[256,512]{1,0:T(8,128)(2,1)S(1)} %copy-done.4, bf16[832,128]{1,0:T(8,128)(2,1)S(1)} %bitcast.9, bf16[512,2048]{1,0:T(8,128)(2,1)S(1)} %copy-done), custom_call_target="tpu_custom_call" | custom-call | tf_op jit(solution)/shard_map/solve/pallas_call | solution.py:248
  66.0 18.6 %all_to_all.23 = bf16[4,256,512]{2,1,0:T(8,128)(2,1)S(1)} all-to-all(bf16[4,256,512]{2,1,0:T(8,128)(2,1)S(1)} %solve.1), channel_id=1, replica_groups=mesh['y'=4,'far'=4,'near'=4,'core'=2,'head'=4] {'head'}, dimensions={0} | all-to-all | bytes 2097152 | tf_op jit(solution)/shard_map/all_to_all | solution.py:257
  84.6 0.8 fusion
Async XLA Ops:
  0.0 61.9 %copy-start = (bf16[512,2048]{1,0:T(8,128)(2,1)S(1)}, bf16[512,2048]{1,0:T(8,128)(2,1)}, u32[]{:S(2)}) copy-start(bf16[512,2048]{1,0:T(8,128)(2,1)} %w_ref.1) | copy-start | bytes 6291460
  0.0 1.1 %copy-start.1 = (bf16[256,512]{1,0:T(8,128)(2,1)S(1)}, bf16[256,512]{1,0:T(8,128)(2,1)}, u32[]{:S(2)}) copy-start(bf16[256,512]{1,0:T(8,128)(2,1)} %k_ref.3) | copy-start | bytes 786436
  1.1 0.9 %copy-start.3 = (bf16[256,512]{1,0:T(8,128)(2,1)S(1)}, bf16[256,512]{1,0:T(8,128)(2,1)}, u32[]{:S(2)}) copy-start(bf16[256,512]{1,0:T(8,128)(2,1)} %v_ref.3) | copy-start | bytes 786436
  2.1 59.8 %copy-start.2 = (bf16[256,512]{1,0:T(8,128)(2,1)S(1)}, bf16[256,512]{1,0:T(8,128)(2,1)}, u32[]{:S(2)}) copy-start(bf16[256,512]{1,0:T(8,128)(2,1)} %k_ref.3) | copy-start | bytes 786436
  2.1 59.9 %copy-start.4 = (bf16[256,512]{1,0:T(8,128)(2,1)S(1)}, bf16[256,512]{1,0:T(8,128)(2,1)}, u32[]{:S(2)}) copy-start(bf16[256,512]{1,0:T(8,128)(2,1)} %v_ref.3) | copy-start | bytes 786436
  2.1 59.9 %copy-start.6 = (f32[4]{0:T(128)S(1)}, f32[4]{0:T(128)}, u32[]{:S(2)}) copy-start(f32[4]{0:T(128)} %ridge_ref.1) | copy-start | bytes 52
  61.9 1.0 %copy-start.5 = (bf16[256,512]{1,0:T(8,128)(2,1)S(1)}, bf16[256,512]{1,0:T(8,128)(2,1)}, u32[]{:S(2)}) copy-start(bf16[256,512]{1,0:T(8,128)(2,1)} %q_ref.1) | copy-start | bytes 786436

commit v5 on v4

--- a/solution.py
+++ b/solution.py
@@ -8,9 +8,11 @@
 
 HD = 128
 SEQ = ("y", "far", "near", "core")
-NEAR = ("y", "near", "core")
 EPS = 1e-06
 ROWS = 4
+Y_ORDER, NEAR_ORDER, CORE_ORDER = (2, 3, 0, 1), (2, 3, 0, 1), (1, 0)
+FAR_ORDER, HEAD_ORDER = (2, 0, 3, 1), (2, 3, 1, 0)
+MEMBERS = [NEAR_ORDER.index(near) * 2 + CORE_ORDER.index(core) for near in range(4) for core in range(2)]
 f32, bf16 = jnp.float32, jnp.bfloat16
 
 
@@ -27,7 +29,14 @@
 
 
 def far_groups():
-    return [[near + 4 * far if far < 2 else (near + 2) % 4 + 4 * far for far in range(4)] for near in range(4)]
+    return [[near + 4 * far if far < 2 else (near + 2) % 4 + 4 * far for far in FAR_ORDER] for near in range(4)]
+
+
+def near_groups():
+    return [
+        [((y * 4 + far) * 4 + near) * 2 + core for y in Y_ORDER for near in NEAR_ORDER for core in CORE_ORDER]
+        for far in range(4)
+    ]
 
 
 def turned(rows, turns):
@@ -67,8 +76,10 @@
     return lax.rsqrt(jnp.sum(keys * keys, axis=1, keepdims=True) + EPS)
 
 
-def grams(k_ref, v_ref, out_ref, rows_ref):
+def grams(k_ref, v_ref, out_ref, keys_ref, values_ref, rows_ref):
     heads = k_ref.shape[1] // HD
+    keys_ref[...] = k_ref[...]
+    values_ref[...] = v_ref[...]
     squares = []
     for h in range(heads):
         cols = slice(h * HD, (h + 1) * HD)
@@ -98,7 +109,7 @@
     piece = total_ref.shape[0] // ROWS
     members = near_ref.shape[0] // total_ref.shape[0]
     for y in range(ROWS):
-        at = y * members * piece
+        at = Y_ORDER.index(y) * members * piece
         total = terms_ref[at : at + piece]
         for member in range(1, members):
             total += terms_ref[at + member * piece : at + (member + 1) * piece]
@@ -112,7 +123,6 @@
     mine = lax.axis_index("far")
     quarters, rows = far_ref.shape[:2]
     piece = rows // ROWS
-    members = terms_ref.shape[0] // rows
     for far in range(quarters):
         total_ref[far * rows : (far + 1) * rows] = unpack(far_ref[far])
     before = jnp.zeros((piece, HD), f32)
@@ -121,10 +131,10 @@
         for far in range(quarters):
             at = far * rows + y * piece
             total = total_ref[at : at + piece]
-            running += jnp.where(far < mine, total, 0.0)
+            running += jnp.where(FAR_ORDER[far] < mine, total, 0.0)
             before += total
-        for member in range(members):
-            at = (y * members + member) * piece
+        for member in MEMBERS:
+            at = (Y_ORDER.index(y) * len(MEMBERS) + member) * piece
             rows_ref[at : at + piece] = running
             running += terms_ref[at : at + piece]
     out_ref[...] = pack(rows_ref[...])
@@ -194,7 +204,8 @@
     mixed = mixed_ref[...]
     piece = out_ref.shape[2]
     for n in range(out_ref.shape[0]):
-        out_ref[n] = dot(mixed, w_ref[:, n * piece : (n + 1) * piece]).astype(bf16)
+        at = HEAD_ORDER[n] * piece
+        out_ref[n] = dot(mixed, w_ref[:, at : at + piece]).astype(bf16)
 
 
 def shards(queries, keys, values, ridges, out_weight):
@@ -206,17 +217,19 @@
 
     def exchange(rows):
         rows = rows.reshape(holders, piece // 2, 2, HD)
-        return lax.all_to_all(rows, NEAR, 0, 0, tiled=True).reshape(holders * piece, HD)
+        rows = lax.all_to_all(rows, SEQ, 0, 0, axis_index_groups=near_groups(), tiled=True)
+        return rows.reshape(holders * piece, HD)
 
     def scratch(count):
         return pltpu.VMEM((count * piece, HD), f32)
 
     rows = jax.ShapeDtypeStruct((holders * piece, HD), bf16)
-    own = pl.pallas_call(
+    held = jax.ShapeDtypeStruct((tokens, width), bf16)
+    own, keys, values = pl.pallas_call(
         grams,
-        out_shape=rows,
+        out_shape=(rows, held, held),
         in_specs=[vmem()] * 2,
-        out_specs=vmem(),
+        out_specs=(vmem(),) * 3,
         scratch_shapes=[scratch(holders)],
         compiler_params=params(),
         name="grams",
@@ -254,7 +267,9 @@
         compiler_params=params(),
         name="solve",
     )(ridges, queries, keys, values, exchange(states), out_weight)
-    partial = lax.all_to_all(partial, "head", 0, 0, tiled=True)
+    partial = lax.all_to_all(
+        partial, "head", 0, 0, axis_index_groups=[HEAD_ORDER], tiled=True
+    )
     total = partial[0].astype(f32)
     for n in range(1, spread):
         total += partial[n].astype(f32)

time: 85.8 us -> 74.7 us (0.87)
  blocking collectives: 77.3 us -> 67.2 us
  local copies, waits for them, and re-layouts: 3.01 us -> 2.06 us
    all_to_all x3, blocking collectives: 57.1 us -> 51 us  [the longest x2 33.5 us: exchange(): lax.all_to_all(rows, SEQ, 0, 0, axis_index_groups=near_groups(), tiled=True)]
    all_to_all x1, blocking collectives: 20.2 us -> 16.1 us  [shards(): lax.all_to_all(totals, ('far', 'near'), 0, 0, axis_index_groups=far_group...]
    unnamed x14 -> x10, local copies, waits for them, and re-layouts: 3.01 us -> 2.06 us
where the time goes in v5:
time: 74.7 us; the launch traced here: 74.4 us
  blocking collectives  67.2 us (90%)
  Pallas kernels  4.31 us (6%)
  local copies, waits for them, and re-layouts  2.06 us (3%)
  other arithmetic  0.84 us (1%)
    all_to_all x2, blocking collectives, exchange(): lax.all_to_all(rows, SEQ, 0, 0, axis_index_groups=near_groups(), tiled=True)  33.5 us
    all_to_all x1, blocking collectives, shards(): lax.all_to_all(partial, 'head', 0, 0, axis_index_groups=[HEAD_ORDER], til...  17.5 us
    all_to_all x1, blocking collectives, shards(): lax.all_to_all(totals, ('far', 'near'), 0, 0, axis_index_groups=far_group...  16.1 us
    pallas_call x1, Pallas kernels, shards(): pl.pallas_call(solve, out_shape=jax.ShapeDtypeStruct((spread, tokens, out...  3.13 us
    unnamed x10, local copies, waits for them, and re-layouts  2.06 us

profile of v5, /device:TPU:1, one launch (start us, length us, event | category | flops | bytes accessed | tf_op | source)
XLA Modules:
  0.0 74.4 jit_solution(836135848053726422)
XLA Ops:
  0.0 0.0 copy-start
  0.0 0.0 copy-start.2
  0.0 1.1 %copy-done.2 = bf16[256,512]{1,0:T(8,128)(2,1)S(1)} copy-done((bf16[256,512]{1,0:T(8,128)(2,1)S(1)}, bf16[256,512]{1,0:T(8,128)(2,1)}, u32[]{:S(2)}) %copy-start.2) | copy-done | bytes 262168
  1.1 0.0 copy-start.3
  1.1 0.9 %copy-done.3 = bf16[256,512]{1,0:T(8,128)(2,1)S(1)} copy-done((bf16[256,512]{1,0:T(8,128)(2,1)S(1)}, bf16[256,512]{1,0:T(8,128)(2,1)}, u32[]{:S(2)}) %copy-start.3) | copy-done | bytes 262168
  2.1 0.0 copy-start.1
  2.1 0.0 copy-start.4
  2.1 0.5 grams.1
  2.6 18.7 %all_to_all.20 = bf16[32,13,2,128]{3,2,1,0:T(2,128)(2,1)S(1)} all-to-all(bf16[32,13,2,128]{3,2,1,0:T(2,128)(2,1)S(1)} %bitcast.9), channel_id=1, replica_groups={{276,272,284,280,260,256,268,264,404,400,412,408,388,384,396,392,20,16,..., dimensions={0} | all-to-all | bytes 425984 | tf_op jit(solution)/shard_map/all_to_all | solution.py:220
  21.3 0.3 group_totals.1
  21.6 16.1 %all_to_all.21.far_ref = bf16[4,104,128]{2,1,0:T(8,128)(2,1)S(1)} all-to-all(bf16[4,104,128]{2,1,0:T(8,128)(2,1)S(1)} %get-tuple-element.14), channel_id=1, replica_groups={{80,0,112,32},{88,8,120,40},{64,16,96,48},{72,24,104,56},{81,1,113,33},..., dimensions={0} | all-to-all | bytes 212992 | tf_op jit(solution)/shard_map/all_to_all | solution.py:249
  37.7 0.3 prefixes.1
  38.0 14.9 %all_to_all.22 = bf16[32,13,2,128]{3,2,1,0:T(2,128)(2,1)S(1)} all-to-all(bf16[32,13,2,128]{3,2,1,0:T(2,128)(2,1)S(1)} %bitcast.7), channel_id=1, replica_groups={{276,272,284,280,260,256,268,264,404,400,412,408,388,384,396,392,20,16,..., dimensions={0} | all-to-all | bytes 425984 | tf_op jit(solution)/shard_map/all_to_all | solution.py:220
  52.9 0.0 copy-done
  52.9 0.0 copy-done.1
  52.9 0.0 copy-done.4
  52.9 3.1 %solve.1 = bf16[4,256,512]{2,1,0:T(8,128)(2,1)S(1)} custom-call(f32[4]{0:T(128)S(1)} %copy-done.4, bf16[256,512]{1,0:T(8,128)(2,1)S(1)} %copy-done.1, bf16[256,512]{1,0:T(8,128)(2,1)S(1)} %get-tuple-element.10.k_ref, bf16[256,512]{1,0:T(8,128)(2,1)S(1)} %get-tuple-element.11.v_ref, bf16[832,128]{1,0:T(8,128)(2,1)S(1)} %bitcast.8, bf16[512,2048]{1,0:T(8,128)(2,1)S(1)} %copy-done), custom_call_target="tpu_custom_call" | custom-call | tf_op jit(solution)/shard_map/solve/pallas_call | solution.py:261
  56.0 17.5 %all_to_all.23 = bf16[4,256,512]{2,1,0:T(8,128)(2,1)S(1)} all-to-all(bf16[4,256,512]{2,1,0:T(8,128)(2,1)S(1)} %solve.1), channel_id=1, replica_groups={{2,3,1,0},{6,7,5,4},{10,11,9,8},{14,15,13,12},{18,19,17,16},{22,23,21,2..., dimensions={0} | all-to-all | bytes 2097152 | tf_op jit(solution)/shard_map/all_to_all | solution.py:270
  73.6 0.8 %fusion = bf16[256,512]{1,0:T(8,128)(2,1)} fusion(bf16[4,256,512]{2,1,0:T(8,128)(2,1)S(1)} %all_to_all.23), kind=kLoop, calls=%fused_computation.1 | loop fusion | flops 1048576 | bytes 1310720 | tf_op jit(solution)/shard_map/add | solution.py:275
Async XLA Ops:
  0.0 52.9 %copy-start = (bf16[512,2048]{1,0:T(8,128)(2,1)S(1)}, bf16[512,2048]{1,0:T(8,128)(2,1)}, u32[]{:S(2)}) copy-start(bf16[512,2048]{1,0:T(8,128)(2,1)} %w_ref.1) | copy-start | bytes 6291460
  0.0 1.1 %copy-start.2 = (bf16[256,512]{1,0:T(8,128)(2,1)S(1)}, bf16[256,512]{1,0:T(8,128)(2,1)}, u32[]{:S(2)}) copy-start(bf16[256,512]{1,0:T(8,128)(2,1)} %k_ref.1) | copy-start | bytes 786436
  1.1 0.9 %copy-start.3 = (bf16[256,512]{1,0:T(8,128)(2,1)S(1)}, bf16[256,512]{1,0:T(8,128)(2,1)}, u32[]{:S(2)}) copy-start(bf16[256,512]{1,0:T(8,128)(2,1)} %v_ref.1) | copy-start | bytes 786436
  2.1 50.8 %copy-start.1 = (bf16[256,512]{1,0:T(8,128)(2,1)S(1)}, bf16[256,512]{1,0:T(8,128)(2,1)}, u32[]{:S(2)}) copy-start(bf16[256,512]{1,0:T(8,128)(2,1)} %q_ref.1) | copy-start | bytes 786436
  2.1 50.8 %copy-start.4 = (f32[4]{0:T(128)S(1)}, f32[4]{0:T(128)}, u32[]{:S(2)}) copy-start(f32[4]{0:T(128)} %ridge_ref.1) | copy-start | bytes 52

commit v6 on v5

--- a/solution.py
+++ b/solution.py
@@ -10,7 +10,7 @@
 SEQ = ("y", "far", "near", "core")
 EPS = 1e-06
 ROWS = 4
-Y_ORDER, NEAR_ORDER, CORE_ORDER = (2, 3, 0, 1), (2, 3, 0, 1), (1, 0)
+Y_ORDER, NEAR_ORDER, CORE_ORDER = (2, 1, 0, 3), (2, 3, 0, 1), (1, 0)
 FAR_ORDER, HEAD_ORDER = (2, 0, 3, 1), (2, 3, 1, 0)
 MEMBERS = [NEAR_ORDER.index(near) * 2 + CORE_ORDER.index(core) for near in range(4) for core in range(2)]
 f32, bf16 = jnp.float32, jnp.bfloat16

time: 74.7 us -> 74.1 us (level)
  no operation moved by 1% of the time
where the time goes in v6:
time: 74.1 us; the launch traced here: 73.9 us
  blocking collectives  66.6 us (90%)
  Pallas kernels  4.31 us (6%)
  local copies, waits for them, and re-layouts  2.06 us (3%)
  other arithmetic  0.84 us (1%)
    all_to_all x2, blocking collectives, exchange(): lax.all_to_all(rows, SEQ, 0, 0, axis_index_groups=near_groups(), tiled=True)  33.7 us
    all_to_all x1, blocking collectives, shards(): lax.all_to_all(partial, 'head', 0, 0, axis_index_groups=[HEAD_ORDER], til...  17.3 us
    all_to_all x1, blocking collectives, shards(): lax.all_to_all(totals, ('far', 'near'), 0, 0, axis_index_groups=far_group...  15.7 us
    pallas_call x1, Pallas kernels, shards(): pl.pallas_call(solve, out_shape=jax.ShapeDtypeStruct((spread, tokens, out...  3.13 us
    unnamed x10, local copies, waits for them, and re-layouts  2.06 us

profile of v6, /device:TPU:1, one launch (start us, length us, event | category | flops | bytes accessed | tf_op | source)
XLA Modules:
  0.0 73.9 jit_solution(14617568654930896170)
XLA Ops:
  0.0 0.0 copy-start
  0.0 0.0 copy-start.2
  0.0 1.1 %copy-done.2 = bf16[256,512]{1,0:T(8,128)(2,1)S(1)} copy-done((bf16[256,512]{1,0:T(8,128)(2,1)S(1)}, bf16[256,512]{1,0:T(8,128)(2,1)}, u32[]{:S(2)}) %copy-start.2) | copy-done | bytes 262168
  1.1 0.0 copy-start.3
  1.1 0.9 %copy-done.3 = bf16[256,512]{1,0:T(8,128)(2,1)S(1)} copy-done((bf16[256,512]{1,0:T(8,128)(2,1)S(1)}, bf16[256,512]{1,0:T(8,128)(2,1)}, u32[]{:S(2)}) %copy-start.3) | copy-done | bytes 262168
  2.1 0.0 copy-start.1
  2.1 0.0 copy-start.4
  2.1 0.5 grams.1
  2.6 18.7 %all_to_all.20 = bf16[32,13,2,128]{3,2,1,0:T(2,128)(2,1)S(1)} all-to-all(bf16[32,13,2,128]{3,2,1,0:T(2,128)(2,1)S(1)} %bitcast.9), channel_id=1, replica_groups={{276,272,284,280,260,256,268,264,148,144,156,152,132,128,140,136,20,16,..., dimensions={0} | all-to-all | bytes 425984 | tf_op jit(solution)/shard_map/all_to_all | solution.py:220
  21.3 0.3 group_totals.1
  21.6 15.7 %all_to_all.21.far_ref = bf16[4,104,128]{2,1,0:T(8,128)(2,1)S(1)} all-to-all(bf16[4,104,128]{2,1,0:T(8,128)(2,1)S(1)} %get-tuple-element.14), channel_id=1, replica_groups={{80,0,112,32},{88,8,120,40},{64,16,96,48},{72,24,104,56},{81,1,113,33},..., dimensions={0} | all-to-all | bytes 212992 | tf_op jit(solution)/shard_map/all_to_all | solution.py:249
  37.3 0.3 prefixes.1
  37.6 15.1 %all_to_all.22 = bf16[32,13,2,128]{3,2,1,0:T(2,128)(2,1)S(1)} all-to-all(bf16[32,13,2,128]{3,2,1,0:T(2,128)(2,1)S(1)} %bitcast.7), channel_id=1, replica_groups={{276,272,284,280,260,256,268,264,148,144,156,152,132,128,140,136,20,16,..., dimensions={0} | all-to-all | bytes 425984 | tf_op jit(solution)/shard_map/all_to_all | solution.py:220
  52.6 0.0 copy-done
  52.6 0.0 copy-done.1
  52.6 0.0 copy-done.4
  52.6 3.1 %solve.1 = bf16[4,256,512]{2,1,0:T(8,128)(2,1)S(1)} custom-call(f32[4]{0:T(128)S(1)} %copy-done.4, bf16[256,512]{1,0:T(8,128)(2,1)S(1)} %copy-done.1, bf16[256,512]{1,0:T(8,128)(2,1)S(1)} %get-tuple-element.10.k_ref, bf16[256,512]{1,0:T(8,128)(2,1)S(1)} %get-tuple-element.11.v_ref, bf16[832,128]{1,0:T(8,128)(2,1)S(1)} %bitcast.8, bf16[512,2048]{1,0:T(8,128)(2,1)S(1)} %copy-done), custom_call_target="tpu_custom_call" | custom-call | tf_op jit(solution)/shard_map/solve/pallas_call | solution.py:261
  55.8 17.3 %all_to_all.23 = bf16[4,256,512]{2,1,0:T(8,128)(2,1)S(1)} all-to-all(bf16[4,256,512]{2,1,0:T(8,128)(2,1)S(1)} %solve.1), channel_id=1, replica_groups={{2,3,1,0},{6,7,5,4},{10,11,9,8},{14,15,13,12},{18,19,17,16},{22,23,21,2..., dimensions={0} | all-to-all | bytes 2097152 | tf_op jit(solution)/shard_map/all_to_all | solution.py:270
  73.0 0.8 %fusion = bf16[256,512]{1,0:T(8,128)(2,1)} fusion(bf16[4,256,512]{2,1,0:T(8,128)(2,1)S(1)} %all_to_all.23), kind=kLoop, calls=%fused_computation.1 | loop fusion | flops 1048576 | bytes 1310720 | tf_op jit(solution)/shard_map/add | solution.py:275
Async XLA Ops:
  0.0 52.6 %copy-start = (bf16[512,2048]{1,0:T(8,128)(2,1)S(1)}, bf16[512,2048]{1,0:T(8,128)(2,1)}, u32[]{:S(2)}) copy-start(bf16[512,2048]{1,0:T(8,128)(2,1)} %w_ref.1) | copy-start | bytes 6291460
  0.0 1.1 %copy-start.2 = (bf16[256,512]{1,0:T(8,128)(2,1)S(1)}, bf16[256,512]{1,0:T(8,128)(2,1)}, u32[]{:S(2)}) copy-start(bf16[256,512]{1,0:T(8,128)(2,1)} %k_ref.1) | copy-start | bytes 786436
  1.1 0.9 %copy-start.3 = (bf16[256,512]{1,0:T(8,128)(2,1)S(1)}, bf16[256,512]{1,0:T(8,128)(2,1)}, u32[]{:S(2)}) copy-start(bf16[256,512]{1,0:T(8,128)(2,1)} %v_ref.1) | copy-start | bytes 786436
  2.1 50.6 %copy-start.1 = (bf16[256,512]{1,0:T(8,128)(2,1)S(1)}, bf16[256,512]{1,0:T(8,128)(2,1)}, u32[]{:S(2)}) copy-start(bf16[256,512]{1,0:T(8,128)(2,1)} %q_ref.1) | copy-start | bytes 786436
  2.1 50.6 %copy-start.4 = (f32[4]{0:T(128)S(1)}, f32[4]{0:T(128)}, u32[]{:S(2)}) copy-start(f32[4]{0:T(128)} %ridge_ref.1) | copy-start | bytes 52

commit v7 on v6

--- a/solution.py
+++ b/solution.py
@@ -10,6 +10,7 @@
 SEQ = ("y", "far", "near", "core")
 EPS = 1e-06
 ROWS = 4
+SPARE = 8
 Y_ORDER, NEAR_ORDER, CORE_ORDER = (2, 1, 0, 3), (2, 3, 0, 1), (1, 0)
 FAR_ORDER, HEAD_ORDER = (2, 0, 3, 1), (2, 3, 1, 0)
 MEMBERS = [NEAR_ORDER.index(near) * 2 + CORE_ORDER.index(core) for near in range(4) for core in range(2)]
@@ -105,16 +106,18 @@
 
 
 def group_totals(near_ref, out_ref, terms_ref, total_ref):
-    terms_ref[...] = unpack(near_ref[...])
-    piece = total_ref.shape[0] // ROWS
-    members = near_ref.shape[0] // total_ref.shape[0]
+    count = near_ref.shape[0]
+    terms_ref[:count] = unpack(near_ref[...])
+    terms_ref[count:] = jnp.zeros((SPARE, HD), f32)
+    piece = out_ref.shape[1] // ROWS
+    members = count // out_ref.shape[1]
     for y in range(ROWS):
         at = Y_ORDER.index(y) * members * piece
         total = terms_ref[at : at + piece]
         for member in range(1, members):
             total += terms_ref[at + member * piece : at + (member + 1) * piece]
         total_ref[y * piece : (y + 1) * piece] = total
-    total = pack(total_ref[...])
+    total = pack(total_ref[: out_ref.shape[1]])
     for far in range(out_ref.shape[0]):
         out_ref[far] = total
 
@@ -137,7 +140,7 @@
             at = (Y_ORDER.index(y) * len(MEMBERS) + member) * piece
             rows_ref[at : at + piece] = running
             running += terms_ref[at : at + piece]
-    out_ref[...] = pack(rows_ref[...])
+    out_ref[...] = pack(rows_ref[: out_ref.shape[0]])
 
 
 def solve(ridge_ref, q_ref, k_ref, v_ref, state_ref, w_ref, out_ref, mixed_ref, rows_ref):
@@ -220,8 +223,8 @@
         rows = lax.all_to_all(rows, SEQ, 0, 0, axis_index_groups=near_groups(), tiled=True)
         return rows.reshape(holders * piece, HD)
 
-    def scratch(count):
-        return pltpu.VMEM((count * piece, HD), f32)
+    def scratch(count, spare=0):
+        return pltpu.VMEM((count * piece + spare, HD), f32)
 
     rows = jax.ShapeDtypeStruct((holders * piece, HD), bf16)
     held = jax.ShapeDtypeStruct((tokens, width), bf16)
@@ -238,11 +241,11 @@
         group_totals,
         out_shape=(
             jax.ShapeDtypeStruct((quarters, ROWS * piece, HD), bf16),
-            jax.ShapeDtypeStruct(rows.shape, f32),
+            jax.ShapeDtypeStruct((holders * piece + SPARE, HD), f32),
         ),
         in_specs=[vmem()],
         out_specs=(vmem(), vmem()),
-        scratch_shapes=[scratch(ROWS)],
+        scratch_shapes=[scratch(ROWS, SPARE)],
         compiler_params=params(),
         name="group_totals",
     )(exchange(own))
@@ -254,7 +257,7 @@
         out_shape=rows,
         in_specs=[vmem(), vmem()],
         out_specs=vmem(),
-        scratch_shapes=[scratch(quarters * ROWS), scratch(holders)],
+        scratch_shapes=[scratch(quarters * ROWS, SPARE), scratch(holders, SPARE)],
         compiler_params=params(),
         name="prefixes",
     )(terms, totals)

time: 74.1 us -> 74.2 us (level)
  no operation moved by 1% of the time
where the time goes in v7:
time: 74.2 us; the launch traced here: 73.9 us
  blocking collectives  66.7 us (90%)
  Pallas kernels  4.3 us (6%)
  local copies, waits for them, and re-layouts  2.06 us (3%)
  other arithmetic  0.84 us (1%)
    all_to_all x2, blocking collectives, exchange(): lax.all_to_all(rows, SEQ, 0, 0, axis_index_groups=near_groups(), tiled=True)  33.7 us
    all_to_all x1, blocking collectives, shards(): lax.all_to_all(partial, 'head', 0, 0, axis_index_groups=[HEAD_ORDER], til...  17.3 us
    all_to_all x1, blocking collectives, shards(): lax.all_to_all(totals, ('far', 'near'), 0, 0, axis_index_groups=far_group...  15.7 us
    pallas_call x1, Pallas kernels, shards(): pl.pallas_call(solve, out_shape=jax.ShapeDtypeStruct((spread, tokens, out...  3.13 us
    unnamed x10, local copies, waits for them, and re-layouts  2.06 us

profile of v7, /device:TPU:1, one launch (start us, length us, event | category | flops | bytes accessed | tf_op | source)
XLA Modules:
  0.0 73.9 jit_solution(831471095819906249)
XLA Ops:
  0.0 0.0 copy-start
  0.0 0.0 copy-start.2
  0.0 1.1 %copy-done.2 = bf16[256,512]{1,0:T(8,128)(2,1)S(1)} copy-done((bf16[256,512]{1,0:T(8,128)(2,1)S(1)}, bf16[256,512]{1,0:T(8,128)(2,1)}, u32[]{:S(2)}) %copy-start.2) | copy-done | bytes 262168
  1.1 0.0 copy-start.3
  1.1 0.9 %copy-done.3 = bf16[256,512]{1,0:T(8,128)(2,1)S(1)} copy-done((bf16[256,512]{1,0:T(8,128)(2,1)S(1)}, bf16[256,512]{1,0:T(8,128)(2,1)}, u32[]{:S(2)}) %copy-start.3) | copy-done | bytes 262168
  2.1 0.0 copy-start.1
  2.1 0.0 copy-start.4
  2.1 0.5 grams.1
  2.6 18.7 %all_to_all.20 = bf16[32,13,2,128]{3,2,1,0:T(2,128)(2,1)S(1)} all-to-all(bf16[32,13,2,128]{3,2,1,0:T(2,128)(2,1)S(1)} %bitcast.9), channel_id=1, replica_groups={{276,272,284,280,260,256,268,264,148,144,156,152,132,128,140,136,20,16,..., dimensions={0} | all-to-all | bytes 425984 | tf_op jit(solution)/shard_map/all_to_all | solution.py:223
  21.3 0.3 group_totals.1
  21.6 15.7 %all_to_all.21.far_ref = bf16[4,104,128]{2,1,0:T(8,128)(2,1)S(1)} all-to-all(bf16[4,104,128]{2,1,0:T(8,128)(2,1)S(1)} %get-tuple-element.14), channel_id=1, replica_groups={{80,0,112,32},{88,8,120,40},{64,16,96,48},{72,24,104,56},{81,1,113,33},..., dimensions={0} | all-to-all | bytes 212992 | tf_op jit(solution)/shard_map/all_to_all | solution.py:252
  37.3 0.3 prefixes.1
  37.6 15.1 %all_to_all.22 = bf16[32,13,2,128]{3,2,1,0:T(2,128)(2,1)S(1)} all-to-all(bf16[32,13,2,128]{3,2,1,0:T(2,128)(2,1)S(1)} %bitcast.7), channel_id=1, replica_groups={{276,272,284,280,260,256,268,264,148,144,156,152,132,128,140,136,20,16,..., dimensions={0} | all-to-all | bytes 425984 | tf_op jit(solution)/shard_map/all_to_all | solution.py:223
  52.6 0.0 copy-done
  52.6 0.0 copy-done.1
  52.6 0.0 copy-done.4
  52.6 3.1 %solve.1 = bf16[4,256,512]{2,1,0:T(8,128)(2,1)S(1)} custom-call(f32[4]{0:T(128)S(1)} %copy-done.4, bf16[256,512]{1,0:T(8,128)(2,1)S(1)} %copy-done.1, bf16[256,512]{1,0:T(8,128)(2,1)S(1)} %get-tuple-element.10.k_ref, bf16[256,512]{1,0:T(8,128)(2,1)S(1)} %get-tuple-element.11.v_ref, bf16[832,128]{1,0:T(8,128)(2,1)S(1)} %bitcast.8, bf16[512,2048]{1,0:T(8,128)(2,1)S(1)} %copy-done), custom_call_target="tpu_custom_call" | custom-call | tf_op jit(solution)/shard_map/solve/pallas_call | solution.py:264
  55.8 17.3 %all_to_all.23 = bf16[4,256,512]{2,1,0:T(8,128)(2,1)S(1)} all-to-all(bf16[4,256,512]{2,1,0:T(8,128)(2,1)S(1)} %solve.1), channel_id=1, replica_groups={{2,3,1,0},{6,7,5,4},{10,11,9,8},{14,15,13,12},{18,19,17,16},{22,23,21,2..., dimensions={0} | all-to-all | bytes 2097152 | tf_op jit(solution)/shard_map/all_to_all | solution.py:273
  73.1 0.8 %fusion = bf16[256,512]{1,0:T(8,128)(2,1)} fusion(bf16[4,256,512]{2,1,0:T(8,128)(2,1)S(1)} %all_to_all.23), kind=kLoop, calls=%fused_computation.1 | loop fusion | flops 1048576 | bytes 1310720 | tf_op jit(solution)/shard_map/add | solution.py:278
Async XLA Ops:
  0.0 52.6 %copy-start = (bf16[512,2048]{1,0:T(8,128)(2,1)S(1)}, bf16[512,2048]{1,0:T(8,128)(2,1)}, u32[]{:S(2)}) copy-start(bf16[512,2048]{1,0:T(8,128)(2,1)} %w_ref.1) | copy-start | bytes 6291460
  0.0 1.1 %copy-start.2 = (bf16[256,512]{1,0:T(8,128)(2,1)S(1)}, bf16[256,512]{1,0:T(8,128)(2,1)}, u32[]{:S(2)}) copy-start(bf16[256,512]{1,0:T(8,128)(2,1)} %k_ref.1) | copy-start | bytes 786436
  1.1 0.9 %copy-start.3 = (bf16[256,512]{1,0:T(8,128)(2,1)S(1)}, bf16[256,512]{1,0:T(8,128)(2,1)}, u32[]{:S(2)}) copy-start(bf16[256,512]{1,0:T(8,128)(2,1)} %v_ref.1) | copy-start | bytes 786436
  2.1 50.6 %copy-start.1 = (bf16[256,512]{1,0:T(8,128)(2,1)S(1)}, bf16[256,512]{1,0:T(8,128)(2,1)}, u32[]{:S(2)}) copy-start(bf16[256,512]{1,0:T(8,128)(2,1)} %q_ref.1) | copy-start | bytes 786436
  2.1 50.6 %copy-start.4 = (f32[4]{0:T(128)S(1)}, f32[4]{0:T(128)}, u32[]{:S(2)}) copy-start(f32[4]{0:T(128)} %ridge_ref.1) | copy-start | bytes 52
